TPU v7x, 256 devices: a whole 4x4x8 slice. The times are simulated.
256 devices in a mesh: seq: 64 (over y, z, core), feat: 4 (over x).
Axes of the slice: x: 4, y: 4, z: 8, core: 2. Of those that a mesh axis runs over, the one named last changes fastest.
Arguments:
- events: bfloat16 [4, 32768, 1024], P('feat', 'seq'), may hold values from -8 to 8
- segment_ids: int32 [4, 32768], P('feat', 'seq'), may hold values from 0 to 15, never falling along the last dimension, each value on 1 to 16384 neighbouring positions
- event_mask: int32 [4, 32768], P('feat', 'seq'), may hold values 0 or 1
- nonseq: bfloat16 [64, 512], P('seq'), may hold values from -6 to 6
- seed_tokens: bfloat16 [16, 1024], replicated, may hold values from -8 to 8
- w_query: bfloat16 [1024, 1024], replicated, may hold values from -1 to 1
- w_key: bfloat16 [1024, 1024], replicated, may hold values from -1 to 1
- w_value: bfloat16 [1024, 1024], replicated, may hold values from -0.1875 to 0.1875
- w_out: bfloat16 [1024, 1024], replicated, may hold values from -0.1875 to 0.1875
- w_pers: bfloat16 [512, 1024], replicated, may hold values from -0.25 to 0.25
- w_comp: bfloat16 [1024, 512], replicated, may hold values from -0.1875 to 0.1875
- w_down: bfloat16 [8192, 128], P('feat'), may hold values from -0.0625 to 0.0625
- w_up: bfloat16 [128, 8192], P(None, 'feat'), may hold values from -0.5 to 0.5
- cross_bias: bfloat16 [8192], P('feat'), may hold values from -3 to 3
Outputs:
- tokens_out: float32 [4, 32768, 1024], P('feat', 'seq')
- cross_out: float32 [64, 8192], P('seq', 'feat')
Inputs may be any that keep to these rules, and one draw needn't show every extreme that they name: `segment_ids`: within a group the ids never fall along the events, every id from 0 to 15 occurs, no user has more than 16384 events, and in every draw some user has exactly 16384.
All inputs are finite; a program needn't handle non-finite values. No bound on the sum of `event_mask` on one device may be relied on, other than what follows from the above.
Results may differ from a plain program's by a relative error of at most 0.015.
The roundings to bfloat16 on the way count: a program that leaves them out, or rounds other values in their place, can miss the bound.
Values may be sent and summed in bfloat16 or wider, within the bound.
No kernel may reach another device: no remote copies, remote signals or barrier semaphores. Data moves between devices by JAX's collectives and lax.ppermute only.
A program may use at most 192 MiB of HBM per device.

v0:
```python
import jax
import jax.numpy as jnp
from jax import lax
from jax.sharding import PartitionSpec as P

HEADS = 8


HIGHEST = lax.Precision.HIGHEST
NEGATIVE = -1e30


def passed_along(value, axis, by):
    peers = lax.axis_size(axis)
    pairs = [(i, i + by) for i in range(peers) if 0 <= i + by < peers]
    return lax.ppermute(value, axis, pairs)


def broadcast(block, axis, owner):
    block = jnp.where(lax.axis_index(axis) == owner, block, jnp.zeros_like(block))
    return lax.psum(block, axis)


def user_sums(member_mask, weights, hidden, head_count, seed_count):
    row_count = weights.shape[0]
    user_count = member_mask.shape[1]
    spread = jnp.where(
        member_mask[:, :, None],
        weights.astype(jnp.bfloat16)[:, None, :],
        jnp.zeros((), jnp.bfloat16),
    )
    spread = spread.reshape(row_count, user_count, seed_count, head_count)
    hidden_heads = hidden.reshape(row_count, head_count, -1)
    result = jnp.einsum("eush,ehd->ushd", spread, hidden_heads, preferred_element_type=jnp.float32)
    return result.reshape(user_count, seed_count * head_count, -1)


def normalize_rows(pooled):
    return (pooled * lax.rsqrt(jnp.mean(pooled * pooled, -1, keepdims=True) + 1e-06)).astype(
        jnp.bfloat16
    )


def local(
    events,
    segment_ids,
    event_mask,
    nonseq,
    seed_tokens,
    w_query,
    w_key,
    w_value,
    w_out,
    w_pers,
    w_comp,
    w_down,
    w_up,
    cross_bias,
):
    tokens = events[0]
    segments = segment_ids[0]
    kept_flags = event_mask[0]
    row_count = tokens.shape[0]
    model_width = tokens.shape[1]
    head_dim = model_width // HEADS
    score_scale = head_dim ** (-0.5)
    group_users = lax.axis_size("seq") // lax.axis_size("feat")
    seq_index = lax.axis_index("seq")
    feat_index = lax.axis_index("feat")
    queries = jnp.dot(tokens, w_query, preferred_element_type=jnp.float32).astype(jnp.bfloat16)
    key_rows = jnp.dot(tokens, w_key, preferred_element_type=jnp.float32).astype(jnp.bfloat16)
    value_rows = jnp.dot(tokens, w_value, preferred_element_type=jnp.float32).astype(jnp.bfloat16)
    prior_keys, prior_values, prior_segments, prior_flags = passed_along(
        (key_rows, value_rows, segments, kept_flags), "seq", 1
    )
    prior_segments = jnp.where(seq_index > 0, prior_segments, -1)
    all_keys = jnp.concatenate([prior_keys, key_rows], 0).reshape(2 * row_count, HEADS, head_dim)
    all_values = jnp.concatenate([prior_values, value_rows], 0).reshape(
        2 * row_count, HEADS, head_dim
    )
    all_segments = jnp.concatenate([prior_segments, segments], 0)
    all_flags = jnp.concatenate([prior_flags, kept_flags], 0)
    query_heads = queries.reshape(row_count, HEADS, head_dim)
    scores = (
        jnp.einsum("qhd,khd->hqk", query_heads, all_keys, preferred_element_type=jnp.float32)
        * score_scale
    )
    query_pos = jnp.arange(row_count, dtype=jnp.int32)[:, None]
    key_pos = jnp.arange(2 * row_count, dtype=jnp.int32)[None, :]
    allowed = (
        (segments[:, None] == all_segments[None, :])
        & (key_pos > query_pos)
        & (key_pos <= query_pos + row_count)
        & ((all_flags[None, :] == 1) | (key_pos == query_pos + row_count))
    )
    masked = jnp.where(allowed[None], scores, NEGATIVE)
    row_top = jnp.max(masked, -1, keepdims=True)
    att_weights = jnp.exp(masked - row_top)
    att_total = jnp.sum(att_weights, -1)
    mixed_sum = jnp.einsum(
        "hqk,khd->qhd",
        att_weights.astype(jnp.bfloat16),
        all_values,
        preferred_element_type=jnp.float32,
    )
    context = (
        (mixed_sum / jnp.transpose(att_total)[:, :, None])
        .astype(jnp.bfloat16)
        .reshape(row_count, model_width)
    )
    full_out = tokens.astype(jnp.float32) + jnp.dot(
        context, w_out, preferred_element_type=jnp.float32
    )
    hidden = full_out.astype(jnp.bfloat16)
    previous = jnp.concatenate([prior_segments[-1:], segments[:-1]], 0)
    usable = (kept_flags == 1) | (segments != previous)
    profiles = lax.all_gather(nonseq, "seq", axis=0, tiled=True)
    group_rows = lax.dynamic_slice_in_dim(profiles, feat_index * group_users, group_users, 0)
    personal = jnp.dot(group_rows, w_pers, preferred_element_type=jnp.float32).astype(jnp.bfloat16)
    user_query = jnp.dot(personal, w_query, preferred_element_type=jnp.float32).astype(jnp.bfloat16)
    seed_query = jnp.dot(seed_tokens, w_query, preferred_element_type=jnp.float32).astype(
        jnp.bfloat16
    )
    seed_count = seed_tokens.shape[0]
    own_keys = key_rows.reshape(row_count, HEADS, head_dim)
    event_query = user_query[segments].reshape(row_count, HEADS, head_dim)
    seed_part = jnp.einsum(
        "ehd,shd->esh",
        own_keys,
        seed_query.reshape(seed_count, HEADS, head_dim),
        preferred_element_type=jnp.float32,
    )
    user_part = jnp.einsum("ehd,ehd->eh", own_keys, event_query, preferred_element_type=jnp.float32)
    flat_score = ((seed_part + user_part[:, None, :]) * score_scale).reshape(
        row_count, seed_count * HEADS
    )
    onehot = segments[:, None] == jnp.arange(group_users, dtype=jnp.int32)[None, :]
    members = onehot & usable[:, None]
    local_peak = jnp.max(
        jnp.where(jnp.transpose(members)[:, :, None], flat_score[None], NEGATIVE), 1
    )
    member_real = onehot.astype(jnp.float32)
    shift_peak = lax.pmax(local_peak, "seq")
    pool_weights = jnp.where(usable[:, None], jnp.exp(flat_score - shift_peak[segments]), 0.0)
    totals = jnp.dot(jnp.transpose(member_real), pool_weights, precision=HIGHEST)
    weighted = user_sums(onehot, pool_weights, hidden, HEADS, seed_count)
    totals, weighted = (totals, weighted)
    totals, weighted = lax.psum((totals, weighted), "seq")
    pooled = (weighted / totals[:, :, None]).reshape(group_users, seed_count, model_width)
    summary = normalize_rows(pooled)
    own_summary = lax.dynamic_index_in_dim(summary, seq_index % group_users, 0, keepdims=False)
    context_line = (
        jnp.dot(own_summary, w_comp, preferred_element_type=jnp.float32)
        .astype(jnp.bfloat16)
        .reshape(1, -1)
    )
    context_line = broadcast(context_line, "feat", seq_index // group_users)
    block_width = context_line.shape[1] // lax.axis_size("feat")
    own_piece = lax.dynamic_slice_in_dim(context_line, feat_index * block_width, block_width, 1)
    rank_terms = jnp.dot(own_piece, w_down, preferred_element_type=jnp.float32)
    rank_part = lax.psum(rank_terms, "feat").astype(jnp.bfloat16)
    lifted = jnp.dot(rank_part, w_up, preferred_element_type=jnp.float32)
    base_row = own_piece.astype(jnp.float32)
    cross_out = base_row * (lifted + cross_bias.astype(jnp.float32)[None, :]) + base_row
    return (full_out[None], cross_out)


def solution(mesh):
    return jax.shard_map(
        local,
        mesh=mesh,
        in_specs=(
            P("feat", "seq", None),
            P("feat", "seq"),
            P("feat", "seq"),
            P("seq", None),
            P(),
            P(),
            P(),
            P(),
            P(),
            P(),
            P(),
            P("feat", None),
            P(None, "feat"),
            P("feat"),
        ),
        out_specs=(P("feat", "seq", None), P("seq", "feat")),
        check_vma=False,
    )
```

profile of v0, /device:TPU:38, one launch (start us, length us, event | category | flops | bytes accessed | tf_op | source)
XLA Modules:
  0.0 472.5 jit_solution(8907336762741210468)
XLA Ops:
  7.2 2.1 collective-permute-start.1
  9.3 4.2 collective-permute-start.2
  13.5 4.2 convolution_convert_fusion
  17.7 2.0 collective-permute-start.3
  19.7 2.3 convolution_convert_fusion.2
  22.0 3.9 collective-permute-start
  26.0 2.2 fusion.18
  28.2 55.3 %all-gather = bf16[64,1,512]{2,1,0:T(2,128)(2,1)S(1)} all-gather(bf16[1,1,512]{2,1,0:T(2,128)(2,1)S(1)} %bitcast.138), channel_id=1, replica_groups=mesh['seq'=64,'feat'=4] {'seq'}, dimensions={0}, use_global_device_ids=true | all-gather | bytes 66560 | tf_op jit(solution)/shard_map/all_gather | solution.py:117
  84.2 2.1 gather_fusion
  89.2 1.6 fusion.23
  93.8 123.4 %pmax.7 = f32[16,128]{1,0:T(8,128)S(1)} all-reduce(f32[16,128]{1,0:T(8,128)S(1)} %select_reduce_fusion), channel_id=1, replica_groups=mesh['seq'=64,'feat'=4] {'seq'}, use_global_device_ids=true, to_apply=%region_3.4 | all-reduce | flops 2048 | bytes 16384 | tf_op jit(solution)/shard_map/pmax | solution.py:143
  219.5 3.0 pad_maximum_fusion
  222.6 4.0 copy.70
  226.5 6.6 %fusion = (f32[8,512]{1,0:T(8,128)S(1)}, f32[8,512,1024]{2,1,0:T(8,128)S(1)}) fusion(pred[512,1024]{1,0:T(8,128)(4,1)S(1)} %fusion.15, bf16[64,8,8,128]{3,2,1,0:T(8,128)(2,1)} %fusion.18, bf16[512,1024]{1,0:T(8,128)(2,1)} %convolution_convert_fusion, bf16[512,1024]{1,0:T(8,128)(2,1)} %collective-permute-done.3), kind=kOutput, calls=%fused_computation.4 | convolution fusion | flops 1090514944 | bytes 20463616 | tf_op jit(solution)/shard_map/qhd,khd->hqk/dot_general | solution.py:85
  233.2 4.5 fusion.1
  237.7 7.4 %fusion.10 = bf16[512,8,128]{0,2,1:T(8,128)(2,1)} fusion(f32[512,8]{0,1:T(8,128)S(1)} %bitcast.133, bf16[1024,8,128]{0,2,1:T(8,128)(2,1)} %bitcast.117, f32[8,512,1024]{2,1,0:T(8,128)S(1)} %get-tuple-element.5, f32[8,512]{1,0:T(8,128)S(1)} %get-tuple-element.4, pred[512,1024]{1,0:T(8,128)(4,1)S(1)} %fusion.15), kind=kOutput, calls=%fused_computation.18 | convolution fusion | flops 1091567616 | bytes 20480000 | tf_op jit(solution)/shard_map/hqk,khd->qhd/dot_general | solution.py:100
  245.2 2.8 convert_add_fusion
  250.1 1.7 copy.117
  252.1 126.2 %psum.29 = f32[16,128]{1,0:T(8,128)S(1)} all-reduce(f32[16,128]{1,0:T(8,128)S(1)} %fusion.40), channel_id=1, replica_groups=mesh['seq'=64,'feat'=4] {'seq'}, use_global_device_ids=true, to_apply=%region_5.6 | all-reduce | flops 2048 | bytes 16384 | tf_op jit(solution)/shard_map/psum | solution.py:148
  378.3 55.3 %all-reduce.2.cloned.1.call-done = f32[16,128,128]{2,1,0:T(8,128)} async-done(((f32[16,128,128]{2,1,0:T(8,128)}), f32[16,128,128]{2,1,0:T(8,128)}) %all-reduce.2.cloned.1.call-update) | async-done | bytes 1048592 | tf_op jit(solution)/shard_map/psum | solution.py:148
  433.6 1.9 multiply_reduce_fusion
  436.9 1.5 fusion.26
  438.5 14.1 %psum.30 = bf16[1,8192]{1,0:T(2,128)(2,1)S(1)} all-reduce(bf16[1,8192]{1,0:T(2,128)(2,1)S(1)} %bitcast.130), channel_id=1, replica_groups=mesh['seq'=64,'feat'=4] {'feat'}, use_global_device_ids=true, to_apply=%region_8.9 | all-reduce | flops 8192 | bytes 32768 | tf_op jit(solution)/shard_map/psum | solution.py:21
  453.8 10.0 %psum.31 = bf16[1,128]{1,0:T(2,128)(2,1)S(1)} all-reduce(f32[1,128]{1,0:T(1,128)S(1)} %fusion.53), channel_id=1, replica_groups=mesh['seq'=64,'feat'=4] {'feat'}, use_global_device_ids=true, to_apply=%region_9.10 | all-reduce | flops 128 | bytes 768 | tf_op jit(solution)/shard_map/psum | solution.py:161
  (67 shorter events, 15.6 us)
Async XLA Ops:
  7.2 18.8 %copy-start = (bf16[1024,1024]{1,0:T(8,128)(2,1)S(1)}, bf16[1024,1024]{1,0:T(8,128)(2,1)}, u32[]{:S(2)}) copy-start(bf16[1024,1024]{1,0:T(8,128)(2,1)} %param.19) | copy-start | bytes 6291460
  7.2 426.4 %all-reduce.2.cloned.1.call-start = ((), (), s32[]{:S(2)}) async-start(), calls=%async_computation | async-start | bytes 2097152 | tf_op jit(solution)/shard_map/psum | solution.py:148
  7.2 83.9 %collective-permute-start.1 = (s32[512]{0:T(512)}, s32[512]{0:T(512)S(1)}, u32[]{:S(2)}, u32[]{:S(2)}) collective-permute-start(s32[512]{0:T(512)} %bitcast.122), channel_id=1, source_target_pairs={{0,4},{4,8},{8,12},{12,16},{16,20},{20,24},{24,28},{28,32},{32,36}... | collective-permute-start | bytes 6152 | tf_op jit(solution)/shard_map/ppermute | solution.py:16
  9.3 10.4 %copy-start.4 = (bf16[1,512,1024]{2,1,0:T(8,128)(2,1)S(1)}, bf16[1,512,1024]{2,1,0:T(8,128)(2,1)}, u32[]{:S(2)}) copy-start(bf16[1,512,1024]{2,1,0:T(8,128)(2,1)} %param.14) | copy-start | bytes 3145732
  9.3 10.4 %copy-start.10 = (bf16[1024,1024]{1,0:T(8,128)(2,1)S(1)}, bf16[1024,1024]{1,0:T(8,128)(2,1)}, u32[]{:S(2)}) copy-start(bf16[1024,1024]{1,0:T(8,128)(2,1)} %param.21) | copy-start | bytes 6291460
  9.3 209.1 %collective-permute-start.2 = (s32[512]{0:T(512)}, s32[512]{0:T(512)S(1)}, u32[]{:S(2)}, u32[]{:S(2)}) collective-permute-start(s32[512]{0:T(512)} %bitcast.134), channel_id=1, source_target_pairs={{0,4},{4,8},{8,12},{12,16},{16,20},{20,24},{24,28},{28,32},{32,36}... | collective-permute-start | bytes 6152 | tf_op jit(solution)/shard_map/ppermute | solution.py:16
  17.7 8.3 %copy-start.5 = (s32[1,512]{1,0:T(1,128)S(1)}, s32[1,512]{1,0:T(1,128)}, u32[]{:S(2)}) copy-start(s32[1,512]{1,0:T(1,128)} %param.15) | copy-start | bytes 6148
  17.7 208.9 %collective-permute-start.3 = (bf16[512,1024]{1,0:T(8,128)(2,1)}, bf16[512,1024]{1,0:T(8,128)(2,1)}, u32[]{:S(2)}, u32[]{:S(2)}) collective-permute-start(bf16[512,1024]{1,0:T(8,128)(2,1)} %convolution_convert_fusion), channel_id=1, source_target_pairs={{0,4},{4,8},{8,12},{12,16},{16,20},{20,24},{24,28},{28,32},{32,36}... | collective-permute-start | bytes 3145736 | tf_op jit(solution)/shard_map/ppermute | solution.py:16
  22.0 197.5 %collective-permute-start = (bf16[512,1024]{1,0:T(8,128)(2,1)}, bf16[512,1024]{1,0:T(8,128)(2,1)}, u32[]{:S(2)}, u32[]{:S(2)}) collective-permute-start(bf16[512,1024]{1,0:T(8,128)(2,1)} %convolution_convert_fusion.2), channel_id=1, source_target_pairs={{0,4},{4,8},{8,12},{12,16},{16,20},{20,24},{24,28},{28,32},{32,36}... | collective-permute-start | bytes 3145736 | tf_op jit(solution)/shard_map/ppermute | solution.py:16
  26.0 2.3 copy-start.9
  26.0 57.6 %copy-start.3 = (bf16[512,1024]{1,0:T(8,128)(2,1)S(1)}, bf16[512,1024]{1,0:T(8,128)(2,1)}, u32[]{:S(2)}) copy-start(bf16[512,1024]{1,0:T(8,128)(2,1)} %param.23) | copy-start | bytes 3145732
  86.5 2.3 copy-start.6
  88.8 2.9 copy-start.7
  237.7 7.5 %copy-start.2 = (bf16[1024,1024]{1,0:T(8,128)(2,1)S(1)}, bf16[1024,1024]{1,0:T(8,128)(2,1)}, u32[]{:S(2)}) copy-start(bf16[1024,1024]{1,0:T(8,128)(2,1)} %param.22) | copy-start | bytes 6291460
  248.0 1.3 copy-start.1
  435.5 29.5 %copy-start.8 = (bf16[2048]{0:T(1024)(128)(2,1)S(1)}, bf16[2048]{0:T(1024)(128)(2,1)}, u32[]{:S(2)}) copy-start(bf16[2048]{0:T(1024)(128)(2,1)} %param.27) | copy-start | bytes 12292
Sparse Core Ops, SparseCore 0:
  251.9 181.7 all-reduce.1
where the time goes:
time: 477 us; the launch traced here: 472 us
  blocking collectives  329 us (69%)
  waiting for transfers between devices  55.4 us (12%)
  matrix products  33.1 us (7%)
  between operations  14.5 us (3%)
  other arithmetic  14.2 us (3%)
  local copies, waits for them, and re-layouts  14.1 us (3%)
  starting transfers between devices  12.2 us (3%)
    psum x1, blocking collectives, local(): totals, weighted = lax.psum((totals, weighted), 'seq')  126 us
    pmax x1, blocking collectives, local(): shift_peak = lax.pmax(local_peak, 'seq')  123 us
    psum x1, waiting for transfers between devices, local(): totals, weighted = lax.psum((totals, weighted), 'seq')  55.3 us
    all_gather x1, blocking collectives, local(): profiles = lax.all_gather(nonseq, 'seq', axis=0, tiled=True)  55.3 us
    psum x1, blocking collectives, broadcast(): return lax.psum(block, axis)  14.1 us
    ppermute x4, starting transfers between devices, passed_along(): return lax.ppermute(value, axis, pairs)  12.2 us
    psum x1, blocking collectives, local(): rank_part = lax.psum(rank_terms, 'feat').astype(jnp.bfloat16)  10 us
  transfers between devices with their start and end apart: 5, of which 1 were waited for; matrix products, arithmetic and copies ran while one was open for 6% of the time, Pallas kernels for 0%

commit v1 on v0

v1 whole, which is shorter than its diff:
```python
import functools
import jax
import jax.numpy as jnp
from jax import lax
from jax.experimental import pallas as pl
from jax.experimental.pallas import tpu as pltpu
from jax.sharding import Mesh, PartitionSpec as P

HEADS = 8
HEAD_DIM = 128
SEEDS = 16
USERS = 16
ROWS = 512
WIDTH = 1024
CHUNK = 256
PAIR = 256
EXTRA = 128
MESSAGE = WIDTH + EXTRA
NEGATIVE = -1e30
ABSENT = -1e29
LOG2E = 1.4426950408889634
SCALE = HEAD_DIM**-0.5 * LOG2E
F32 = jnp.float32
BF16 = jnp.bfloat16


def dot(a, b):
    return jnp.dot(a, b, preferred_element_type=F32)


def dot_rows(a, b):
    return lax.dot_general(a, b, (((1,), (1,)), ((), ())), preferred_element_type=F32)


def same_user(query_segments, key_segments, key_flags):
    ids = lax.broadcasted_iota(jnp.int32, (USERS, ROWS), 0)
    left = jnp.where(query_segments == ids, 1.0, 0.0).astype(BF16)
    right = jnp.where((key_segments == ids) & (key_flags == 1), 1.0, 0.0).astype(BF16)
    match = lax.dot_general(left, right, (((0,), (0,)), ((), ())), preferred_element_type=F32)
    return match > 0.5


def own_body(x_ref, seg_ref, flag_ref, wq_ref, wk_ref, wv_ref, q_ref, k_ref, acc_ref, ml_ref, bias_ref):
    @pl.when(pl.program_id(0) == 0)
    def _():
        row = lax.broadcasted_iota(jnp.int32, (ROWS, ROWS), 0)
        col = lax.broadcasted_iota(jnp.int32, (ROWS, ROWS), 1)
        same = same_user(seg_ref[...], seg_ref[...], flag_ref[...])
        bias_ref[...] = jnp.where((same & (col < row)) | (col == row), 0.0, NEGATIVE)

    x = x_ref[...]
    q = dot(x, wq_ref[...]).astype(BF16)
    k = dot(x, wk_ref[...]).astype(BF16)
    v = dot(x, wv_ref[...]).astype(BF16)
    q_ref[...] = q
    k_ref[...] = k
    lane = lax.broadcasted_iota(jnp.int32, (CHUNK, 128), 1)
    for at in range(0, ROWS, CHUNK):
        end = at + CHUNK
        stats = jnp.zeros((CHUNK, 128), F32)
        for half in range(PAIR // HEAD_DIM):
            cols = slice(half * HEAD_DIM, (half + 1) * HEAD_DIM)
            score = dot_rows(q[at:end, cols], k[:end, cols]) * SCALE + bias_ref[at:end, :end]
            top = jnp.max(score, 1, keepdims=True)
            weight = jnp.exp2(score - top)
            total = jnp.sum(weight, 1, keepdims=True)
            acc_ref[at:end, cols] = dot(weight.astype(BF16), v[:end, cols])
            stats = jnp.where(lane == half, top, jnp.where(lane == half + 2, total, stats))
        ml_ref[0, at:end, :] = stats


def prior_body(
    xp_ref, x_ref, seg_ref, segp_ref, flagp_ref, wk_ref, wv_ref, wo_ref, q_ref, acc_ref, ml_ref,
    out_ref, hid_ref, bias_ref,
):
    step = pl.program_id(0)

    @pl.when(step == 0)
    def _():
        row = lax.broadcasted_iota(jnp.int32, (ROWS, ROWS), 0)
        col = lax.broadcasted_iota(jnp.int32, (ROWS, ROWS), 1)
        same = same_user(seg_ref[...], segp_ref[...], flagp_ref[...])
        bias_ref[...] = jnp.where(same & (col > row), 0.0, NEGATIVE)
        out_ref[...] = x_ref[...].astype(F32)

    xp = xp_ref[...]
    k = dot(xp, wk_ref[...]).astype(BF16)
    v = dot(xp, wv_ref[...]).astype(BF16)
    for at in range(0, ROWS, CHUNK):
        end = at + CHUNK
        parts = []
        for half in range(PAIR // HEAD_DIM):
            cols = slice(half * HEAD_DIM, (half + 1) * HEAD_DIM)
            score = dot_rows(q_ref[at:end, cols], k[at:, cols]) * SCALE + bias_ref[at:end, at:]
            before = ml_ref[0, at:end, half : half + 1]
            total = ml_ref[0, at:end, half + 2 : half + 3]
            top = jnp.maximum(before, jnp.max(score, 1, keepdims=True))
            weight = jnp.exp2(score - top)
            shrink = jnp.exp2(before - top)
            total = total * shrink + jnp.sum(weight, 1, keepdims=True)
            mixed = acc_ref[at:end, cols] * shrink + dot(weight.astype(BF16), v[at:, cols])
            parts.append((mixed / total).astype(BF16))
        out_ref[at:end, :] += dot(jnp.concatenate(parts, 1), wo_ref[...])

    @pl.when(step == pl.num_programs(0) - 1)
    def _():
        hid_ref[...] = out_ref[...].astype(BF16)


def split_terms(stats, lane):
    high = stats.astype(BF16).astype(F32)
    rest = stats - high
    middle = rest.astype(BF16).astype(F32)
    low = rest - middle
    return jnp.where(lane < 16, high, jnp.where(lane < 32, middle, low)).astype(BF16)


def join_terms(extra):
    extra = extra.astype(F32)
    return extra + pltpu.roll(extra, 112, 1) + pltpu.roll(extra, 96, 1)


def pool_body(place_ref, hid_ref, k_ref, sq_ref, uq_ref, seg_ref, segp_ref, flag_ref, keep_ref, send_ref):
    core = place_ref[0]
    own_user = place_ref[1]
    count = USERS * SEEDS
    row = lax.broadcasted_iota(jnp.int32, (count, 16), 0)
    col = lax.broadcasted_iota(jnp.int32, (count, 16), 1)
    user16 = ((row % 32) // 4) * 2 + (core ^ (row // 128))
    seed16 = ((row % 128) // 32) * 4 + row % 4
    pick_seed = jnp.where(col == seed16, 1.0, 0.0).astype(BF16)
    pick_user = jnp.where(col == (user16 ^ own_user), 1.0, 0.0).astype(BF16)
    seeds = dot(pick_seed, sq_ref[...]).astype(BF16)
    users = dot(pick_user, uq_ref[...]).astype(BF16)

    segs = seg_ref[...]
    lanes = lax.broadcasted_iota(jnp.int32, (8, ROWS), 1)
    before = pltpu.roll(jnp.broadcast_to(segs, (8, ROWS)), 1, 1)
    before = jnp.where(lanes == 0, segp_ref[:, ROWS - 1 :], before)
    usable = (flag_ref[...] == 1) | (segs != before[0:1])
    marked = jnp.where(usable, segs, -1)
    wide = lax.broadcasted_iota(jnp.int32, (count, ROWS), 0)
    user_of = ((wide % 32) // 4) * 2 + (core ^ (wide // 128))
    bias = jnp.where(marked == user_of, 0.0, NEGATIVE)

    lane = lax.broadcasted_iota(jnp.int32, (count, 128), 1)
    stats = jnp.zeros((count, 128), F32)
    for head in range(HEADS):
        cols = slice(head * HEAD_DIM, (head + 1) * HEAD_DIM)
        keys = k_ref[:, cols]
        queries = jnp.concatenate([seeds[:, cols], users[:, cols]], 1)
        score = dot_rows(queries, jnp.concatenate([keys, keys], 1)) * SCALE + bias
        top = jnp.maximum(jnp.max(score, 1, keepdims=True), ABSENT)
        weight = jnp.exp2(score - top)
        total = jnp.sum(weight, 1, keepdims=True)
        pooled = dot(weight.astype(BF16), hid_ref[:, cols]).astype(BF16)
        keep_ref[:, cols] = pooled[:128]
        send_ref[:, cols] = pooled[128:]
        place = lane % 16
        stats = jnp.where(place == head, top, jnp.where(place == head + 8, total, stats))
    extra = jnp.where(lane < 48, split_terms(stats, lane), jnp.zeros((), BF16))
    keep_ref[:, WIDTH:] = extra[:128]
    send_ref[:, WIDTH:] = extra[128:]


def merge_body(a_ref, b_ref, out_ref):
    a = join_terms(a_ref[:, WIDTH:])
    b = join_terms(b_ref[:, WIDTH:])
    top = jnp.maximum(a, b)
    scale_a = jnp.exp2(a - top)
    scale_b = jnp.exp2(b - top)
    lane = lax.broadcasted_iota(jnp.int32, a.shape, 1)
    total = a * pltpu.roll(scale_a, 8, 1) + b * pltpu.roll(scale_b, 8, 1)
    stats = jnp.where(lane < 8, top, jnp.where(lane < 16, total, 0.0))
    stats = stats + pltpu.roll(stats, 16, 1) + pltpu.roll(stats, 32, 1)
    out_ref[:, WIDTH:] = jnp.where(lane < 48, split_terms(stats, lane), jnp.zeros((), BF16))
    for head in range(HEADS):
        cols = slice(head * HEAD_DIM, (head + 1) * HEAD_DIM)
        out_ref[:, cols] = (
            a_ref[:, cols].astype(F32) * scale_a[:, head : head + 1]
            + b_ref[:, cols].astype(F32) * scale_b[:, head : head + 1]
        ).astype(BF16)


def finish_body(in_ref, comp_ref, down_ref, row_ref, rank_ref):
    stats = join_terms(in_ref[:, WIDTH:]).reshape(16, 8, 128)
    top = jnp.max(stats, 0)
    top = jnp.maximum(top, pltpu.roll(top, 4, 0))
    scale = jnp.exp2(stats - top[None])
    shifted = pltpu.roll(scale.reshape(128, 128), 8, 1).reshape(16, 8, 128)
    total = jnp.sum(stats * shifted, 0)
    total = total + pltpu.roll(total, 4, 0)
    parts = []
    for head in range(HEADS):
        cols = slice(head * HEAD_DIM, (head + 1) * HEAD_DIM)
        data = in_ref[:, cols].astype(F32).reshape(16, 8, 128)
        part = jnp.sum(data * scale[:, :, head : head + 1], 0)
        part = part + pltpu.roll(part, 4, 0)
        parts.append(part / total[:, head + 8 : head + 9])
    pooled = jnp.concatenate(parts, 1)
    mean = jnp.mean(pooled * pooled, 1, keepdims=True)
    summary = (pooled * lax.rsqrt(mean + 1e-06)).astype(BF16)
    context = dot(summary, comp_ref[...]).astype(BF16)
    rank = jnp.zeros((1, 128), F32)
    for seed in range(4):
        rank = rank + dot(context, down_ref[seed * 512 : (seed + 1) * 512, :])[seed : seed + 1]
    wide = lax.broadcasted_iota(jnp.int32, (8, 512), 0)
    spread = jnp.concatenate([rank] + [jnp.zeros((1, 128), F32)] * 3, 1)
    row_ref[...] = jnp.where(wide < 4, context.astype(F32), spread)
    rank_ref[...] = jnp.broadcast_to(rank, (8, 128))


def cross_body(row_ref, b_ref, c_ref, d_ref, up_ref, bias_ref, out_ref):
    rank = row_ref[4:5, :128] + b_ref[0:1] + c_ref[0:1] + d_ref[0:1]
    rank = jnp.broadcast_to(rank, (8, 128)).astype(BF16)
    lifted = dot(rank, up_ref[...])[0:1]
    base = jnp.concatenate([row_ref[seed : seed + 1, :] for seed in range(4)], 1)
    out_ref[...] = base * (lifted + bias_ref[...].astype(F32)) + base


def shape(dims, dtype):
    return jax.ShapeDtypeStruct(dims, dtype)


def whole():
    return pl.BlockSpec(memory_space=pltpu.VMEM)


def cost(flops, nbytes, exps=0):
    return pl.CostEstimate(flops=flops, bytes_accessed=nbytes, transcendentals=exps)


def params(megabytes):
    return pltpu.CompilerParams(vmem_limit_bytes=megabytes << 20)


def attend_own(x, segs, flags, w_query, w_key, w_value):
    fixed = lambda dims: pl.BlockSpec(dims, lambda i: (0,) * len(dims))
    cols = lambda rows: pl.BlockSpec((rows, PAIR), lambda i: (0, i))
    steps = WIDTH // PAIR
    return pl.pallas_call(
        own_body,
        grid=(steps,),
        in_specs=[fixed((ROWS, WIDTH)), fixed((1, ROWS)), fixed((1, ROWS))] + [cols(WIDTH)] * 3,
        out_specs=[cols(ROWS)] * 3 + [pl.BlockSpec((1, ROWS, 128), lambda i: (i, 0, 0))],
        out_shape=[
            shape((ROWS, WIDTH), BF16),
            shape((ROWS, WIDTH), BF16),
            shape((ROWS, WIDTH), F32),
            shape((steps, ROWS, 128), F32),
        ],
        scratch_shapes=[pltpu.VMEM((ROWS, ROWS), F32)],
        compiler_params=params(32),
        cost_estimate=cost(5 << 30, 12 << 20, 2 << 20),
        name="own",
    )(x, segs, flags, w_query, w_key, w_value)


def attend_prior(xp, x, segs, segp, flagp, w_key, w_value, w_out, q, acc, ml):
    fixed = lambda dims: pl.BlockSpec(dims, lambda i: (0,) * len(dims))
    cols = lambda rows: pl.BlockSpec((rows, PAIR), lambda i: (0, i))
    steps = WIDTH // PAIR
    return pl.pallas_call(
        prior_body,
        grid=(steps,),
        in_specs=[fixed((ROWS, WIDTH))] * 2
        + [fixed((1, ROWS))] * 3
        + [cols(WIDTH)] * 2
        + [pl.BlockSpec((PAIR, WIDTH), lambda i: (i, 0)), cols(ROWS), cols(ROWS)]
        + [pl.BlockSpec((1, ROWS, 128), lambda i: (i, 0, 0))],
        out_specs=[fixed((ROWS, WIDTH))] * 2,
        out_shape=[shape((ROWS, WIDTH), F32), shape((ROWS, WIDTH), BF16)],
        scratch_shapes=[pltpu.VMEM((ROWS, ROWS), F32)],
        compiler_params=params(40),
        cost_estimate=cost(5 << 30, 14 << 20, 2 << 20),
        name="prior",
    )(xp, x, segs, segp, flagp, w_key, w_value, w_out, q, acc, ml)


def call(body, outs, args, specs=None, flops=1 << 28, nbytes=2 << 20, name=None):
    return pl.pallas_call(
        body,
        in_specs=specs or [whole()] * len(args),
        out_specs=[whole()] * len(outs),
        out_shape=outs,
        compiler_params=params(24),
        cost_estimate=cost(flops, nbytes),
        name=name,
    )(*args)


def swap(value, turn=0):
    pairs = [(q * 4 + g, g * 4 + (q + turn) % 4) for q in range(4) for g in range(4)]
    return lax.ppermute(value, ("y", "x"), pairs)


def flip(value, axis, size, bit):
    return lax.ppermute(value, axis, [(i, i ^ bit) for i in range(size)])


def local(
    events, segment_ids, event_mask, nonseq, seed_tokens, w_query, w_key, w_value, w_out, w_pers,
    w_comp, w_down, w_up, cross_bias,
):
    x = events[0]
    first = (lax.axis_index("y") == 0) & (lax.axis_index("z") == 0) & (lax.axis_index("core") == 0)
    core = lax.axis_index("core").astype(jnp.int32)
    own_user = lax.axis_index("z").astype(jnp.int32) * 2 + core
    line = ("y", "z", "core")
    onward = [(i, i + 1) for i in range(63)]
    xp = lax.ppermute(x, line, onward)
    marks = lax.ppermute(jnp.concatenate([segment_ids, event_mask], 0), line, onward)
    segp = jnp.where(first, -1, marks[0:1])
    flagp = marks[1:2]

    users = swap(nonseq)
    users = jnp.concatenate([users, flip(users, "core", 2, 1)], 0)
    for bit in (1, 2, 4):
        users = jnp.concatenate([users, flip(users, "z", 8, bit)], 0)
    down = swap(w_down)

    q, k, acc, ml = attend_own(x, segment_ids, event_mask, w_query, w_key, w_value)
    profile = dot(users, w_pers).astype(BF16)
    user_query = dot(profile, w_query).astype(BF16)
    seed_query = dot(seed_tokens, w_query).astype(BF16)
    out, hidden = attend_prior(
        xp, x, segment_ids, segp, flagp, w_key, w_value, w_out, q, acc, ml
    )
    half = shape((128, MESSAGE), BF16)
    keep, send = call(
        pool_body,
        [half, half],
        [jnp.stack([core, own_user]), hidden, k, seed_query, user_query, segment_ids, segp, event_mask],
        [pl.BlockSpec(memory_space=pltpu.SMEM)] + [whole()] * 7,
        name="pool",
    )
    received = flip(send, "core", 2, 1)
    merged = call(merge_body, [half], [keep, received], name="merge")[0]
    pieces = lax.all_to_all(merged.reshape(32, 4, MESSAGE), ("y", "z"), 0, 0, tiled=True)
    row, rank = call(
        finish_body,
        [shape((8, 512), F32), shape((8, 128), F32)],
        [pieces.reshape(128, MESSAGE), w_comp, down],
        name="finish",
    )
    row = swap(row)
    ranks = [swap(rank, turn) for turn in (1, 2, 3)]
    cross = call(
        cross_body,
        [shape((1, 2048), F32)],
        [row] + ranks + [w_up, cross_bias[None]],
        name="cross",
    )[0]
    return out[None], cross


def solution(mesh):
    split = Mesh(mesh.devices.reshape(4, 8, 2, 4), ("y", "z", "core", "x"))
    seq = ("y", "z", "core")
    return jax.shard_map(
        local,
        mesh=split,
        in_specs=(
            P("x", seq, None), P("x", seq), P("x", seq), P(seq, None),
            P(), P(), P(), P(), P(), P(), P(),
            P("x", None), P(None, "x"), P("x"),
        ),
        out_specs=(P("x", seq, None), P(seq, "x")),
        check_vma=False,
    )
```

time: 477 us -> 143 us (0.30)
  blocking collectives: 329 us -> 0 us
  Pallas kernels: 0 us -> 35.2 us
  matrix products: 33.1 us -> 0.92 us
  starting transfers between devices: 12.2 us -> 43.9 us
  waiting for transfers between devices: 55.4 us -> 36 us
  between operations: 14.5 us -> 0.84 us
  other arithmetic: 14.2 us -> 0.83 us
  local copies, waits for them, and re-layouts: 14.1 us -> 22.3 us
    psum x3 -> x0, blocking collectives: 150 us -> none  [the longest x1 126 us: local(): totals, weighted = lax.psum((totals, weighted), 'seq')]
    pmax x1 -> x0, blocking collectives: 123 us -> none  [local(): shift_peak = lax.pmax(local_peak, 'seq')]
    psum x1 -> x0, waiting for transfers between devices: 55.3 us -> none  [local(): totals, weighted = lax.psum((totals, weighted), 'seq')]
    all_gather x1 -> x0, blocking collectives: 55.3 us -> none  [local(): profiles = lax.all_gather(nonseq, 'seq', axis=0, tiled=True)]
    pallas_call x0 -> x6, Pallas kernels: none -> 35.2 us  [the longest x1 18.5 us: attend_prior(): pl.pallas_call(prior_body, grid=(steps,), in_specs=[fixed((ROWS, WIDTH))]...]
    dot_general x14 -> x2, matrix products: 33.1 us -> 0.92 us  [dot(): return jnp.dot(a, b, preferred_element_type=F32)]
    ppermute x4 -> x13, waiting for transfers between devices: 0.01 us -> 28.9 us  [the longest x6 19.9 us: swap(): return lax.ppermute(value, ('y', 'x'), pairs)]
    ppermute x4 -> x13, starting transfers between devices: 12.2 us -> 35.8 us  [the longest x6 20.3 us: swap(): return lax.ppermute(value, ('y', 'x'), pairs)]
  transfers between devices with their start and end apart: 5 -> 14, of which waited for: 1 -> 7; matrix products, arithmetic and copies ran while one was open for 6% -> 2% of each run, Pallas kernels for 0% -> 8%
where the time goes in v1:
time: 143 us; the launch traced here: 140 us
  starting transfers between devices  43.9 us (31%)
  waiting for transfers between devices  36 us (25%)
  Pallas kernels  35.2 us (25%)
  local copies, waits for them, and re-layouts  22.3 us (16%)
    unnamed x52, local copies, waits for them, and re-layouts  20.4 us
    ppermute x6, starting transfers between devices, swap(): return lax.ppermute(value, ('y', 'x'), pairs)  20.3 us
    ppermute x6, waiting for transfers between devices, swap(): return lax.ppermute(value, ('y', 'x'), pairs)  19.9 us
    pallas_call x1, Pallas kernels, attend_prior(): pl.pallas_call(prior_body, grid=(steps,), in_specs=[fixed((ROWS, WIDTH))]...  18.5 us
    pallas_call x1, Pallas kernels, attend_own(): pl.pallas_call(own_body, grid=(steps,), in_specs=[fixed((ROWS, WIDTH)), f...  11.1 us
    ppermute x5, starting transfers between devices, flip(): return lax.ppermute(value, axis, [(i, i ^ bit) for i in range(size)])  9.82 us
    ppermute x5, waiting for transfers between devices, flip(): return lax.ppermute(value, axis, [(i, i ^ bit) for i in range(size)])  9 us
    all_to_all x1, starting transfers between devices, local(): lax.all_to_all(merged.reshape(32, 4, MESSAGE), ('y', 'z'), 0, 0, tiled=True)  8.06 us
  transfers between devices with their start and end apart: 14, of which 7 were waited for; matrix products, arithmetic and copies ran while one was open for 2% of the time, Pallas kernels for 8%

profile of v1, /device:TPU:38, one launch (start us, length us, event | category | flops | bytes accessed | tf_op | source)
XLA Modules:
  0.0 140.0 jit_solution(941725774126050515)
XLA Ops:
  0.6 2.1 %collective-permute-start = (bf16[512,1024]{1,0:T(8,128)(2,1)}, bf16[512,1024]{1,0:T(8,128)(2,1)}, u32[]{:S(2)}, u32[]{:S(2)}) collective-permute-start(bf16[512,1024]{1,0:T(8,128)(2,1)} %bitcast.9), channel_id=1, source_target_pairs={{0,4},{4,8},{8,12},{12,16},{16,20},{20,24},{24,28},{28,32},{32,36}... | collective-permute-start | bytes 3145736 | tf_op jit(solution)/shard_map/ppermute | solution.py:311
  2.7 4.8 %collective-permute-start.2 = (bf16[1,512]{1,0:T(2,128)(2,1)}, bf16[1,512]{1,0:T(2,128)(2,1)S(1)}, u32[]{:S(2)}, u32[]{:S(2)}) collective-permute-start(bf16[1,512]{1,0:T(2,128)(2,1)} %param.17), channel_id=1, source_target_pairs={{0,0},{1,64},{2,128},{3,192},{64,1},{65,65},{66,129},{67,193},{128... | collective-permute-start | bytes 3080 | tf_op jit(solution)/shard_map/ppermute | solution.py:294
  8.3 3.6 %collective-permute-start.1 = (s32[2,512]{1,0:T(2,128)S(1)}, s32[2,512]{1,0:T(2,128)S(1)}, u32[]{:S(2)}, u32[]{:S(2)}) collective-permute-start(s32[2,512]{1,0:T(2,128)S(1)} %pad_add_fusion), channel_id=1, source_target_pairs={{0,4},{4,8},{8,12},{12,16},{16,20},{20,24},{24,28},{28,32},{32,36}... | collective-permute-start | bytes 12296 | tf_op jit(solution)/shard_map/ppermute | solution.py:312
  12.6 1.6 %copy-done.1 = bf16[1024,1024]{1,0:T(8,128)(2,1)S(1)} copy-done((bf16[1024,1024]{1,0:T(8,128)(2,1)S(1)}, bf16[1024,1024]{1,0:T(8,128)(2,1)}, u32[]{:S(2)}) %copy-start.1) | copy-done | bytes 2097176
  15.5 1.6 %copy-done.10 = bf16[1024,1024]{1,0:T(8,128)(2,1)S(1)} copy-done((bf16[1024,1024]{1,0:T(8,128)(2,1)S(1)}, bf16[1024,1024]{1,0:T(8,128)(2,1)}, u32[]{:S(2)}) %copy-start.10) | copy-done | bytes 2097176
  17.1 1.6 %copy-done.12 = bf16[1024,1024]{1,0:T(8,128)(2,1)S(1)} copy-done((bf16[1024,1024]{1,0:T(8,128)(2,1)S(1)}, bf16[1024,1024]{1,0:T(8,128)(2,1)}, u32[]{:S(2)}) %copy-start.12) | copy-done | bytes 2097176
  20.0 11.1 %own.1 = (bf16[512,1024]{1,0:T(8,128)(2,1)S(1)}, bf16[512,1024]{1,0:T(8,128)(2,1)S(1)}, f32[512,1024]{1,0:T(8,128)S(1)}, f32[4,512,128]{2,1,0:T(8,128)S(1)}) custom-call(bf16[512,1024]{1,0:T(8,128)(2,1)S(1)} %bitcast.10, s32[1,512]{1,0:T(1,128)S(1)} %copy-done.6, s32[1,512]{1,0:T(1,128)S(1)} %copy-done.8, bf16[1024,1024]{1,0:T(8,128)(2,1)S(1)} %copy-done.1, ...), custom_call_target="tpu_custom_call" | custom-call | flops 5368709120 | bytes 12582912 | tf_op jit(solution)/shard_map/own/pallas_call | solution.py:241
  34.7 2.3 %collective-permute-done.4 = bf16[2,512]{1,0:T(2,128)(2,1)S(1)} collective-permute-done((bf16[2,512]{1,0:T(2,128)(2,1)S(1)}, bf16[2,512]{1,0:T(2,128)(2,1)S(1)}, u32[]{:S(2)}, u32[]{:S(2)}) %collective-permute-start.4) | collective-permute-done | bytes 2080 | tf_op jit(solution)/shard_map/ppermute | solution.py:298
  37.1 4.6 %collective-permute-start.5 = (bf16[4,512]{1,0:T(4,128)(2,1)S(1)}, bf16[4,512]{1,0:T(4,128)(2,1)S(1)}, u32[]{:S(2)}, u32[]{:S(2)}) collective-permute-start(bf16[4,512]{1,0:T(4,128)(2,1)S(1)} %pad_maximum_fusion.1), channel_id=1, source_target_pairs={{0,16},{8,24},{16,0},{24,8},{32,48},{40,56},{48,32},{56,40},{1,17}... | collective-permute-start | bytes 12296 | tf_op jit(solution)/shard_map/ppermute | solution.py:298
  43.3 4.1 %collective-permute-start.6 = (bf16[8,512]{1,0:T(8,128)(2,1)S(1)}, bf16[8,512]{1,0:T(8,128)(2,1)S(1)}, u32[]{:S(2)}, u32[]{:S(2)}) collective-permute-start(bf16[8,512]{1,0:T(8,128)(2,1)S(1)} %pad_maximum_fusion), channel_id=1, source_target_pairs={{0,32},{8,40},{16,48},{24,56},{32,0},{40,8},{48,16},{56,24},{1,33}... | collective-permute-start | bytes 24584 | tf_op jit(solution)/shard_map/ppermute | solution.py:298
  47.3 3.6 %collective-permute-done.6 = bf16[8,512]{1,0:T(8,128)(2,1)S(1)} collective-permute-done((bf16[8,512]{1,0:T(8,128)(2,1)S(1)}, bf16[8,512]{1,0:T(8,128)(2,1)S(1)}, u32[]{:S(2)}, u32[]{:S(2)}) %collective-permute-start.6) | collective-permute-done | bytes 8224 | tf_op jit(solution)/shard_map/ppermute | solution.py:298
  51.5 1.6 %copy-done.11 = bf16[1024,1024]{1,0:T(8,128)(2,1)S(1)} copy-done((bf16[1024,1024]{1,0:T(8,128)(2,1)S(1)}, bf16[1024,1024]{1,0:T(8,128)(2,1)}, u32[]{:S(2)}) %copy-start.11) | copy-done | bytes 2097176
  53.1 1.6 %copy-done.13 = bf16[1024,1024]{1,0:T(8,128)(2,1)S(1)} copy-done((bf16[1024,1024]{1,0:T(8,128)(2,1)S(1)}, bf16[1024,1024]{1,0:T(8,128)(2,1)}, u32[]{:S(2)}) %copy-start.13) | copy-done | bytes 2097176
  54.7 1.6 %copy-done.14 = bf16[1024,1024]{1,0:T(8,128)(2,1)S(1)} copy-done((bf16[1024,1024]{1,0:T(8,128)(2,1)S(1)}, bf16[1024,1024]{1,0:T(8,128)(2,1)}, u32[]{:S(2)}) %copy-start.14) | copy-done | bytes 2097176
  57.5 1.6 %copy-done.19 = f32[512,1024]{1,0:T(8,128)S(1)} copy-done((f32[512,1024]{1,0:T(8,128)S(1)}, f32[512,1024]{1,0:T(8,128)}, u32[]{:S(2)}) %copy-start.19) | copy-done | bytes 2097176
  61.6 18.5 %prior.1 = (f32[512,1024]{1,0:T(8,128)}, bf16[512,1024]{1,0:T(8,128)(2,1)S(1)}) custom-call(bf16[512,1024]{1,0:T(8,128)(2,1)} %collective-permute-done.xp_ref, bf16[512,1024]{1,0:T(8,128)(2,1)S(1)} %bitcast.11, s32[1,512]{1,0:T(1,128)S(1)} %copy-done.7, s32[1,512]{1,0:T(1,128)S(1)} %get-tuple-element.23.segp_ref, s32[1,512]{1,0:T(1,128)S(1)} %get-tuple-element.22.flagp_ref, ...), custom_call_target="tpu_custom_call" | custom-call | flops 5368709120 | bytes 14680064 | tf_op jit(solution)/shard_map/prior/pallas_call | solution.py:263
  80.1 3.4 %pool.1 = (bf16[128,1152]{1,0:T(8,128)(2,1)S(1)}, bf16[128,1152]{1,0:T(8,128)(2,1)S(1)}) custom-call(s32[2]{0:T(128)S(1)} %pad_add_fusion.1.place_ref, bf16[512,1024]{1,0:T(8,128)(2,1)S(1)} %get-tuple-element.16.hid_ref, bf16[512,1024]{1,0:T(8,128)(2,1)S(1)} %copy-done.5, bf16[16,1024]{1,0:T(8,128)(2,1)S(1)} %convolution_convert_fusion.2.sq_ref, ...), custom_call_target="tpu_custom_call" | custom-call | flops 268435456 | bytes 2097152 | tf_op jit(solution)/shard_map/pool/pallas_call | solution.py:281
  86.7 8.1 %all-to-all-start = ((bf16[32,4,1152]{2,1,0:T(4,128)(2,1)}), bf16[32,4,1152]{2,1,0:T(4,128)(2,1)}, u32[]{:S(2)}, u32[]{:S(2)}) async-start(bf16[32,4,1152]{2,1,0:T(4,128)(2,1)} %reshape.10), calls=%async_computation | async-start | bytes 589824 | tf_op jit(solution)/shard_map/all_to_all | solution.py:339
  94.8 6.2 %collective-permute-start.8 = (bf16[2048,128]{1,0:T(8,128)(2,1)}, bf16[2048,128]{1,0:T(8,128)(2,1)S(1)}, u32[]{:S(2)}, u32[]{:S(2)}) collective-permute-start(bf16[2048,128]{1,0:T(8,128)(2,1)} %param.25), channel_id=1, source_target_pairs={{0,0},{1,64},{2,128},{3,192},{64,1},{65,65},{66,129},{67,193},{128... | collective-permute-start | bytes 1572872 | tf_op jit(solution)/shard_map/ppermute | solution.py:294
  100.9 7.2 %all-to-all-done = bf16[32,4,1152]{2,1,0:T(4,128)(2,1)} async-done(((bf16[32,4,1152]{2,1,0:T(4,128)(2,1)}), bf16[32,4,1152]{2,1,0:T(4,128)(2,1)}, u32[]{:S(2)}, u32[]{:S(2)}) %all-to-all-start) | async-done | bytes 294944 | tf_op jit(solution)/shard_map/all_to_all | solution.py:339
  109.2 15.7 %collective-permute-done.8.down_ref = bf16[2048,128]{1,0:T(8,128)(2,1)S(1)} collective-permute-done((bf16[2048,128]{1,0:T(8,128)(2,1)}, bf16[2048,128]{1,0:T(8,128)(2,1)S(1)}, u32[]{:S(2)}, u32[]{:S(2)}) %collective-permute-start.8) | collective-permute-done | bytes 524320 | tf_op jit(solution)/shard_map/ppermute | solution.py:294
  125.7 6.2 %collective-permute-start.9 = (f32[8,512]{1,0:T(8,128)S(1)}, f32[8,512]{1,0:T(8,128)S(1)}, u32[]{:S(2)}, u32[]{:S(2)}) collective-permute-start(f32[8,512]{1,0:T(8,128)S(1)} %get-tuple-element.20), channel_id=1, source_target_pairs={{0,0},{1,64},{2,128},{3,192},{64,1},{65,65},{66,129},{67,193},{128... | collective-permute-start | bytes 49160 | tf_op jit(solution)/shard_map/ppermute | solution.py:294
  133.4 1.6 %collective-permute-start.12 = (f32[8,128]{1,0:T(8,128)S(1)}, f32[8,128]{1,0:T(8,128)S(1)}, u32[]{:S(2)}, u32[]{:S(2)}) collective-permute-start(f32[8,128]{1,0:T(8,128)S(1)} %get-tuple-element.21), channel_id=1, source_target_pairs={{0,3},{1,67},{2,131},{3,195},{64,0},{65,64},{66,128},{67,192},{128... | collective-permute-start | bytes 12296 | tf_op jit(solution)/shard_map/ppermute | solution.py:294
  135.0 4.2 %collective-permute-done.10.b_ref = f32[8,128]{1,0:T(8,128)S(1)} collective-permute-done((f32[8,128]{1,0:T(8,128)S(1)}, f32[8,128]{1,0:T(8,128)S(1)}, u32[]{:S(2)}, u32[]{:S(2)}) %collective-permute-start.10) | collective-permute-done | bytes 4128 | tf_op jit(solution)/shard_map/ppermute | solution.py:294
  (74 shorter events, 21.0 us)
Async XLA Ops:
  0.6 50.3 %copy-start = (bf16[512,1024]{1,0:T(8,128)(2,1)S(1)}, bf16[512,1024]{1,0:T(8,128)(2,1)}, u32[]{:S(2)}) copy-start(bf16[512,1024]{1,0:T(8,128)(2,1)} %param.23) | copy-start | bytes 3145732
  0.6 50.9 %collective-permute-start = (bf16[512,1024]{1,0:T(8,128)(2,1)}, bf16[512,1024]{1,0:T(8,128)(2,1)}, u32[]{:S(2)}, u32[]{:S(2)}) collective-permute-start(bf16[512,1024]{1,0:T(8,128)(2,1)} %bitcast.9), channel_id=1, source_target_pairs={{0,4},{4,8},{8,12},{12,16},{16,20},{20,24},{24,28},{28,32},{32,36}... | collective-permute-start | bytes 3145736 | tf_op jit(solution)/shard_map/ppermute | solution.py:311
  2.7 9.2 %collective-permute-start.2 = (bf16[1,512]{1,0:T(2,128)(2,1)}, bf16[1,512]{1,0:T(2,128)(2,1)S(1)}, u32[]{:S(2)}, u32[]{:S(2)}) collective-permute-start(bf16[1,512]{1,0:T(2,128)(2,1)} %param.17), channel_id=1, source_target_pairs={{0,0},{1,64},{2,128},{3,192},{64,1},{65,65},{66,129},{67,193},{128... | collective-permute-start | bytes 3080 | tf_op jit(solution)/shard_map/ppermute | solution.py:294
  8.3 39.1 %collective-permute-start.1 = (s32[2,512]{1,0:T(2,128)S(1)}, s32[2,512]{1,0:T(2,128)S(1)}, u32[]{:S(2)}, u32[]{:S(2)}) collective-permute-start(s32[2,512]{1,0:T(2,128)S(1)} %pad_add_fusion), channel_id=1, source_target_pairs={{0,4},{4,8},{8,12},{12,16},{16,20},{20,24},{24,28},{28,32},{32,36}... | collective-permute-start | bytes 12296 | tf_op jit(solution)/shard_map/ppermute | solution.py:312
  11.9 21.5 %collective-permute-start.3 = (bf16[1,512]{1,0:T(2,128)(2,1)S(1)}, bf16[1,512]{1,0:T(2,128)(2,1)S(1)}, u32[]{:S(2)}, u32[]{:S(2)}) collective-permute-start(bf16[1,512]{1,0:T(2,128)(2,1)S(1)} %collective-permute-done.2), channel_id=1, source_target_pairs={{0,4},{4,0},{1,5},{5,1},{2,6},{6,2},{3,7},{7,3},{8,12},{12,8},{9,1... | collective-permute-start | bytes 3080 | tf_op jit(solution)/shard_map/ppermute | solution.py:298
  20.0 13.7 %copy-start.24 = (bf16[16,1024]{1,0:T(8,128)(2,1)S(1)}, bf16[16,1024]{1,0:T(8,128)(2,1)}, u32[]{:S(2)}) copy-start(bf16[16,1024]{1,0:T(8,128)(2,1)} %param.18) | copy-start | bytes 98308
  33.4 17.6 %copy-start.2 = (bf16[1024,1024]{1,0:T(8,128)(2,1)S(1)}, bf16[1024,1024]{1,0:T(8,128)(2,1)}, u32[]{:S(2)}) copy-start(bf16[1024,1024]{1,0:T(8,128)(2,1)} %wq_ref.1) | copy-start | bytes 6291460
  33.4 3.7 %collective-permute-start.4 = (bf16[2,512]{1,0:T(2,128)(2,1)S(1)}, bf16[2,512]{1,0:T(2,128)(2,1)S(1)}, u32[]{:S(2)}, u32[]{:S(2)}) collective-permute-start(bf16[2,512]{1,0:T(2,128)(2,1)S(1)} %pad_maximum_fusion.2), channel_id=1, source_target_pairs={{0,8},{8,0},{16,24},{24,16},{32,40},{40,32},{48,56},{56,48},{1,9},... | collective-permute-start | bytes 6152 | tf_op jit(solution)/shard_map/ppermute | solution.py:298
  34.7 16.8 %copy-start.7 = (s32[1,512]{1,0:T(1,128)S(1)}, s32[1,512]{1,0:T(1,128)}, u32[]{:S(2)}) copy-start(s32[1,512]{1,0:T(1,128)} %seg_ref.5) | copy-start | bytes 6148
  37.1 6.2 %collective-permute-start.5 = (bf16[4,512]{1,0:T(4,128)(2,1)S(1)}, bf16[4,512]{1,0:T(4,128)(2,1)S(1)}, u32[]{:S(2)}, u32[]{:S(2)}) collective-permute-start(bf16[4,512]{1,0:T(4,128)(2,1)S(1)} %pad_maximum_fusion.1), channel_id=1, source_target_pairs={{0,16},{8,24},{16,0},{24,8},{32,48},{40,56},{48,32},{56,40},{1,17}... | collective-permute-start | bytes 12296 | tf_op jit(solution)/shard_map/ppermute | solution.py:298
  43.3 7.6 %collective-permute-start.6 = (bf16[8,512]{1,0:T(8,128)(2,1)S(1)}, bf16[8,512]{1,0:T(8,128)(2,1)S(1)}, u32[]{:S(2)}, u32[]{:S(2)}) collective-permute-start(bf16[8,512]{1,0:T(8,128)(2,1)S(1)} %pad_maximum_fusion), channel_id=1, source_target_pairs={{0,32},{8,40},{16,48},{24,56},{32,0},{40,8},{48,16},{56,24},{1,33}... | collective-permute-start | bytes 24584 | tf_op jit(solution)/shard_map/ppermute | solution.py:298
  51.5 1.6 %copy-start.11 = (bf16[1024,1024]{1,0:T(8,128)(2,1)S(1)}, bf16[1024,1024]{1,0:T(8,128)(2,1)}, u32[]{:S(2)}) copy-start(bf16[1024,1024]{1,0:T(8,128)(2,1)} %wk_ref.3) | copy-start | bytes 6291460
  61.6 18.5 %copy-start.5 = (bf16[512,1024]{1,0:T(8,128)(2,1)S(1)}, bf16[512,1024]{1,0:T(8,128)(2,1)}, u32[]{:S(2)}) copy-start(bf16[512,1024]{1,0:T(8,128)(2,1)} %copy-done.4) | copy-start | bytes 3145732
  61.6 18.5 %copy-start.9 = (s32[1,512]{1,0:T(1,128)S(1)}, s32[1,512]{1,0:T(1,128)}, u32[]{:S(2)}) copy-start(s32[1,512]{1,0:T(1,128)} %flag_ref.3) | copy-start | bytes 6148
  80.1 44.7 %copy-start.3 = (bf16[1024,512]{1,0:T(8,128)(2,1)S(1)}, bf16[1024,512]{1,0:T(8,128)(2,1)}, u32[]{:S(2)}) copy-start(bf16[1024,512]{1,0:T(8,128)(2,1)} %comp_ref.1) | copy-start | bytes 3145732
  83.5 1.9 %collective-permute-start.7 = (bf16[128,1152]{1,0:T(8,128)(2,1)S(1)}, bf16[128,1152]{1,0:T(8,128)(2,1)S(1)}, u32[]{:S(2)}, u32[]{:S(2)}) collective-permute-start(bf16[128,1152]{1,0:T(8,128)(2,1)S(1)} %get-tuple-element.19), channel_id=1, source_target_pairs={{0,4},{4,0},{1,5},{5,1},{2,6},{6,2},{3,7},{7,3},{8,12},{12,8},{9,1... | collective-permute-start | bytes 884744 | tf_op jit(solution)/shard_map/ppermute | solution.py:298
  85.3 49.7 %copy-start.25 = (bf16[2048]{0:T(1024)(128)(2,1)S(1)}, bf16[2048]{0:T(1024)(128)(2,1)}, u32[]{:S(2)}) copy-start(bf16[2048]{0:T(1024)(128)(2,1)} %param.27) | copy-start | bytes 12292
  85.3 53.9 %copy-start.17 = (bf16[128,2048]{1,0:T(8,128)(2,1)S(1)}, bf16[128,2048]{1,0:T(8,128)(2,1)}, u32[]{:S(2)}) copy-start(bf16[128,2048]{1,0:T(8,128)(2,1)} %up_ref.1) | copy-start | bytes 1572868
  86.7 21.4 %all-to-all-start = ((bf16[32,4,1152]{2,1,0:T(4,128)(2,1)}), bf16[32,4,1152]{2,1,0:T(4,128)(2,1)}, u32[]{:S(2)}, u32[]{:S(2)}) async-start(bf16[32,4,1152]{2,1,0:T(4,128)(2,1)} %reshape.10), calls=%async_computation | async-start | bytes 589824 | tf_op jit(solution)/shard_map/all_to_all | solution.py:339
  94.8 30.1 %collective-permute-start.8 = (bf16[2048,128]{1,0:T(8,128)(2,1)}, bf16[2048,128]{1,0:T(8,128)(2,1)S(1)}, u32[]{:S(2)}, u32[]{:S(2)}) collective-permute-start(bf16[2048,128]{1,0:T(8,128)(2,1)} %param.25), channel_id=1, source_target_pairs={{0,0},{1,64},{2,128},{3,192},{64,1},{65,65},{66,129},{67,193},{128... | collective-permute-start | bytes 1572872 | tf_op jit(solution)/shard_map/ppermute | solution.py:294
  125.7 13.5 %collective-permute-start.9 = (f32[8,512]{1,0:T(8,128)S(1)}, f32[8,512]{1,0:T(8,128)S(1)}, u32[]{:S(2)}, u32[]{:S(2)}) collective-permute-start(f32[8,512]{1,0:T(8,128)S(1)} %get-tuple-element.20), channel_id=1, source_target_pairs={{0,0},{1,64},{2,128},{3,192},{64,1},{65,65},{66,129},{67,193},{128... | collective-permute-start | bytes 49160 | tf_op jit(solution)/shard_map/ppermute | solution.py:294
  131.9 7.3 %collective-permute-start.10 = (f32[8,128]{1,0:T(8,128)S(1)}, f32[8,128]{1,0:T(8,128)S(1)}, u32[]{:S(2)}, u32[]{:S(2)}) collective-permute-start(f32[8,128]{1,0:T(8,128)S(1)} %get-tuple-element.21), channel_id=1, source_target_pairs={{0,1},{1,65},{2,129},{3,193},{64,2},{65,66},{66,130},{67,194},{128... | collective-permute-start | bytes 12296 | tf_op jit(solution)/shard_map/ppermute | solution.py:294
  132.0 7.2 %collective-permute-start.11 = (f32[8,128]{1,0:T(8,128)S(1)}, f32[8,128]{1,0:T(8,128)S(1)}, u32[]{:S(2)}, u32[]{:S(2)}) collective-permute-start(f32[8,128]{1,0:T(8,128)S(1)} %get-tuple-element.21), channel_id=1, source_target_pairs={{0,2},{1,66},{2,130},{3,194},{64,3},{65,67},{66,131},{67,195},{128... | collective-permute-start | bytes 12296 | tf_op jit(solution)/shard_map/ppermute | solution.py:294
  133.4 5.8 %collective-permute-start.12 = (f32[8,128]{1,0:T(8,128)S(1)}, f32[8,128]{1,0:T(8,128)S(1)}, u32[]{:S(2)}, u32[]{:S(2)}) collective-permute-start(f32[8,128]{1,0:T(8,128)S(1)} %get-tuple-element.21), channel_id=1, source_target_pairs={{0,3},{1,67},{2,131},{3,195},{64,0},{65,64},{66,128},{67,192},{128... | collective-permute-start | bytes 12296 | tf_op jit(solution)/shard_map/ppermute | solution.py:294
  (16 other events, 20.4 us)

commit v2 on v1

v2 whole, which is shorter than its diff:
```python
import functools
import jax
import jax.numpy as jnp
from jax import lax
from jax.experimental import pallas as pl
from jax.experimental.pallas import tpu as pltpu
from jax.sharding import Mesh, PartitionSpec as P

HEADS = 8
HEAD_DIM = 128
SEEDS = 16
USERS = 16
ROWS = 512
WIDTH = 1024
HALF = 256
CHUNK = 256
PIECE = 512
EXTRA = 128
MESSAGE = WIDTH + EXTRA
SPAN = WIDTH // 2
NEGATIVE = -1e30
ABSENT = -1e29
LOG2E = 1.4426950408889634
SCALE = HEAD_DIM**-0.5 * LOG2E
F32 = jnp.float32
BF16 = jnp.bfloat16


def dot(a, b):
    return jnp.dot(a, b, preferred_element_type=F32)


def dot_rows(a, b):
    return lax.dot_general(a, b, (((1,), (1,)), ((), ())), preferred_element_type=F32)


def same_user(query_segments, key_segments, key_flags):
    def users(ids, kept):
        ones = (ids == lax.broadcasted_iota(jnp.int32, (USERS, ids.shape[1]), 0)) & kept
        return jnp.where(ones, 1.0, 0.0).astype(BF16)

    left = users(query_segments, True)
    right = users(key_segments, key_flags == 1)
    match = lax.dot_general(left, right, (((0,), (0,)), ((), ())), preferred_element_type=F32)
    return match > 0.5


def square(rows, cols):
    row = lax.broadcasted_iota(jnp.int32, (rows, cols), 0)
    return row, lax.broadcasted_iota(jnp.int32, (rows, cols), 1)


def head_cols(head):
    return slice(head * HEAD_DIM, (head + 1) * HEAD_DIM)


def beside_ones(values):
    return jnp.concatenate([values, jnp.ones(values.shape, BF16)], 1)


def load_body(x_hbm, seg_hbm, flag_hbm, high_ref, low_ref, seg_ref, flag_ref, sems):
    quarter = HALF // 2
    copies = [
        pltpu.make_async_copy(seg_hbm, seg_ref, sems.at[0]),
        pltpu.make_async_copy(flag_hbm, flag_ref, sems.at[1]),
    ]
    for start, target in ((HALF, high_ref), (0, low_ref)):
        for at in (0, quarter):
            copies.append(
                pltpu.make_async_copy(
                    x_hbm.at[pl.ds(start + at, quarter)], target.at[pl.ds(at, quarter)], sems.at[len(copies)]
                )
            )
    for copy in copies:
        copy.start()
    copies[0].wait()
    copies[1].wait()
    row, _ = square(16, ROWS)
    marks = jnp.where(row == 0, seg_ref[...], jnp.where(row == 1, flag_ref[...], 0))
    high_ref[HALF:, :ROWS] = marks.astype(F32).astype(BF16)
    high_ref[HALF:, ROWS:] = jnp.zeros((16, WIDTH - ROWS), BF16)
    for copy in copies[2:]:
        copy.wait()


def project_body(
    place_ref, low_ref, high_ref, wq_hbm, wk_hbm, wv_hbm, wo_hbm, seg_ref, flag_ref,
    wq_ref, wk_ref, wv_ref, wo_ref, q_ref, k_ref, v_ref, bias_ref, sems,
):
    copies = []
    triples = [(wq_hbm, wq_ref, q_ref), (wk_hbm, wk_ref, k_ref), (wv_hbm, wv_ref, v_ref)]
    for source, target, _ in triples:
        for at in range(0, WIDTH, PIECE):
            cols = slice(at, at + PIECE)
            copies.append(
                pltpu.make_async_copy(source.at[:, cols], target.at[:, cols], sems.at[len(copies)])
            )
    copies.append(pltpu.make_async_copy(wo_hbm, wo_ref, sems.at[len(copies)]))
    for copy in copies:
        copy.start()
    row, col = square(ROWS, ROWS)
    same = same_user(seg_ref[...], seg_ref[...], flag_ref[...])
    bias_ref[...] = jnp.where((same & (col < row)) | (col == row), 0.0, NEGATIVE)
    x = jnp.concatenate([low_ref[...], high_ref[:HALF]], 0)
    at = 0
    for _, weight, result in triples:
        for start in range(0, WIDTH, PIECE):
            cols = slice(start, start + PIECE)
            copies[at].wait()
            result[:, cols] = dot(x, weight[:, cols]).astype(BF16)
            at += 1
    copies[at].wait()


def query_body(a_ref, b_ref, c_ref, d_ref, e_ref, pers_ref, wq_ref, seed_ref, sq_ref, uq_ref):
    rows = [ref[...].astype(F32) for ref in (a_ref, b_ref, c_ref, d_ref, e_ref)]
    profile = dot(jnp.concatenate(rows, 0).astype(BF16), pers_ref[...])
    both = jnp.concatenate([seed_ref[...].astype(F32), profile], 0).astype(BF16)
    queries = dot(both, wq_ref[...]).astype(BF16)
    sq_ref[...] = queries[:SEEDS]
    uq_ref[...] = queries[SEEDS:]


def own_body(q_ref, k_ref, v_ref, bias_ref, acc_ref, top_ref, total_ref):
    for head in range(HEADS):
        cols = head_cols(head)
        values = beside_ones(v_ref[:, cols])
        for at in range(0, ROWS, CHUNK):
            end = at + CHUNK
            score = dot_rows(q_ref[at:end, cols], k_ref[:end, cols]) * SCALE + bias_ref[at:end, :end]
            top = jnp.max(score, 1, keepdims=True)
            mixed = dot(jnp.exp2(score - top).astype(BF16), values[:end])
            acc_ref[at:end, cols] = mixed[:, :HEAD_DIM]
            total_ref[at:end, cols] = mixed[:, HEAD_DIM:]
            top_ref[at:end, cols] = jnp.broadcast_to(top, (CHUNK, HEAD_DIM))


def absorb(queries, keys, values, bias, mixed, top, total):
    score = dot_rows(queries, keys) * SCALE + bias
    before = top
    top = jnp.maximum(before, jnp.max(score, 1, keepdims=True))
    weights = [
        jnp.exp2(score[:, at : at + HEAD_DIM] - top) for at in range(0, score.shape[1], HEAD_DIM)
    ]
    fresh = dot(jnp.concatenate(weights, 1).astype(BF16), values)
    shrink = jnp.exp2(before - top)
    return mixed * shrink + fresh[:, :HEAD_DIM], top, total * shrink + fresh[:, HEAD_DIM:]


def marks_of(place_ref, near_ref, cols):
    marks = near_ref[HALF:, cols].astype(F32).astype(jnp.int32)
    return jnp.where(place_ref[2] == 1, -1, marks[0:1]), marks[1:2]


def near_body(
    place_ref, xp_ref, wk_ref, wv_ref, wo_ref, x_ref, q_ref, acc_ref, top_ref, total_ref, seg_ref,
    out_ref, hid_ref, acc2_ref, top2_ref, total2_ref, bias_ref, key_ref, value_ref, context_ref,
):
    segp, flagp = marks_of(place_ref, xp_ref, slice(HALF, ROWS))
    row, col = square(ROWS, HALF)
    same = same_user(seg_ref[...], segp, flagp)
    bias_ref[...] = jnp.where(same & (col + HALF > row), 0.0, NEGATIVE)
    xp = xp_ref[:HALF]
    key_ref[...] = dot(xp, wk_ref[...]).astype(BF16)
    value_ref[...] = dot(xp, wv_ref[...]).astype(BF16)
    for head in range(HEADS):
        cols = head_cols(head)
        values = beside_ones(value_ref[:, cols])
        for at in range(0, ROWS, CHUNK):
            end = at + CHUNK
            first = max(at - HALF, 0)
            mixed, top, total = absorb(
                q_ref[at:end, cols], key_ref[first:, cols], values[first:], bias_ref[at:end, first:],
                acc_ref[at:end, cols], top_ref[at:end, cols], total_ref[at:end, cols],
            )
            if at < HALF:
                acc2_ref[at:end, cols] = mixed
                top2_ref[at:end, cols] = top
                total2_ref[at:end, cols] = total
            else:
                context_ref[at - HALF : end - HALF, cols] = (mixed / total).astype(BF16)
    out = x_ref[:HALF].astype(F32) + dot(context_ref[...], wo_ref[...])
    out_ref[...] = out
    hid_ref[...] = out.astype(BF16)


def far_body(
    place_ref, xp_ref, wk_ref, wv_ref, wo_ref, x_ref, q_ref, acc_ref, top_ref, total_ref, seg_ref, marks_ref,
    out_ref, hid_ref, bias_ref, key_ref, value_ref, context_ref,
):
    segp, flagp = marks_of(place_ref, marks_ref, slice(0, HALF))
    row, col = square(HALF, HALF)
    same = same_user(seg_ref[:, :HALF], segp, flagp)
    bias_ref[...] = jnp.where(same & (col > row), 0.0, NEGATIVE)
    xp = xp_ref[...]
    key_ref[...] = dot(xp, wk_ref[...]).astype(BF16)
    value_ref[...] = dot(xp, wv_ref[...]).astype(BF16)
    for head in range(HEADS):
        cols = head_cols(head)
        values = beside_ones(value_ref[:, cols])
        for at in range(0, HALF, CHUNK):
            end = at + CHUNK
            mixed, top, total = absorb(
                q_ref[at:end, cols], key_ref[at:, cols], values[at:], bias_ref[at:end, at:],
                acc_ref[at:end, cols], top_ref[at:end, cols], total_ref[at:end, cols],
            )
            context_ref[at:end, cols] = (mixed / total).astype(BF16)
    out = x_ref[...].astype(F32) + dot(context_ref[...], wo_ref[...])
    out_ref[...] = out
    hid_ref[...] = out.astype(BF16)


def split_terms(stats, width):
    _, lane = square(*stats.shape)
    stats = jnp.where(lane < width, stats, 0.0)
    high = stats.astype(BF16).astype(F32)
    rest = stats - high
    middle = rest.astype(BF16).astype(F32)
    low = rest - middle
    return (high + pltpu.roll(middle, width, 1) + pltpu.roll(low, 2 * width, 1)).astype(BF16)


def join_terms(extra, width):
    extra = extra.astype(F32)
    return extra + pltpu.roll(extra, 128 - width, 1) + pltpu.roll(extra, 128 - 2 * width, 1)


def pool_body(
    place_ref, low_ref, high_ref, hid_low_ref, hid_high_ref, k_ref, sq_ref, uq_ref, seg_ref, marks_ref, flag_ref,
    keep_ref, send_ref, out_hbm, sems,
):
    writes = [
        pltpu.make_async_copy(low_ref, out_hbm.at[pl.ds(0, HALF)], sems.at[0]),
        pltpu.make_async_copy(high_ref, out_hbm.at[pl.ds(HALF, HALF)], sems.at[1]),
    ]
    for write in writes:
        write.start()
    core = place_ref[0]
    own_user = place_ref[1]
    count = USERS * SEEDS
    row, col = square(count, USERS)
    user16 = ((row % 32) // 4) * 2 + (core ^ (row // 128))
    seed16 = ((row % 128) // 32) * 4 + row % 4
    pick_seed = jnp.where(col == seed16, 1.0, 0.0).astype(BF16)
    apart = user16 ^ own_user
    place = (apart & 3) | ((apart & 4) << 1) | ((apart & 8) >> 1)
    pick_user = jnp.where(col == place, 1.0, 0.0).astype(BF16)
    seeds = dot(pick_seed, sq_ref[...]).astype(BF16)
    users = dot(pick_user, uq_ref[...]).astype(BF16)

    segs = seg_ref[...]
    segp, _ = marks_of(place_ref, marks_ref, slice(ROWS - 128, ROWS))
    lanes = lax.broadcasted_iota(jnp.int32, (8, ROWS), 1)
    before = pltpu.roll(jnp.broadcast_to(segs, (8, ROWS)), 1, 1)
    before = jnp.where(lanes == 0, segp[:, 127:], before)
    usable = (flag_ref[...] == 1) | (segs != before[0:1])
    marked = jnp.where(usable, segs, -1)
    wide, _ = square(count, ROWS)
    user_of = ((wide % 32) // 4) * 2 + (core ^ (wide // 128))
    bias = jnp.where(marked == user_of, 0.0, NEGATIVE)

    _, lane = square(count, 128)
    stats = jnp.zeros((count, 128), F32)
    for head in range(HEADS):
        cols = head_cols(head)
        keys = k_ref[:, cols]
        queries = jnp.concatenate([seeds[:, cols], users[:, cols]], 1)
        score = dot_rows(queries, jnp.concatenate([keys, keys], 1)) * SCALE + bias
        top = jnp.maximum(jnp.max(score, 1, keepdims=True), ABSENT)
        weight = jnp.exp2(score - top).astype(BF16)
        pooled = dot(weight[:, :HALF], beside_ones(hid_low_ref[:, cols]))
        pooled = pooled + dot(weight[:, HALF:], beside_ones(hid_high_ref[:, cols]))
        sums = pooled[:, :HEAD_DIM].astype(BF16)
        keep_ref[:, cols] = sums[:128]
        send_ref[:, cols] = sums[128:]
        stats = jnp.where(lane == head, top, jnp.where(lane == head + 8, pooled[:, HEAD_DIM:], stats))
    extra = split_terms(stats, 16)
    keep_ref[:, WIDTH:] = extra[:128]
    send_ref[:, WIDTH:] = extra[128:]
    for write in writes:
        write.wait()


def fold(left, right):
    left = left.reshape(16, 8, 128)
    right = right.reshape(16, 8, 128)
    upper = lax.broadcasted_iota(jnp.int32, left.shape, 1) < 4
    even = jnp.where(upper, left, pltpu.roll(right, 4, 1))
    odd = jnp.where(upper, pltpu.roll(left, 4, 1), right)
    return jnp.stack([even, odd], 1).reshape(256, 128)


def merge_body(a_ref, b_ref, out_ref):
    a = join_terms(a_ref[:, WIDTH:], 16)
    b = join_terms(b_ref[:, WIDTH:], 16)
    top = jnp.maximum(a, b)
    scale_a = jnp.exp2(a - top)
    scale_b = jnp.exp2(b - top)
    _, lane = square(*a.shape)
    total = a * pltpu.roll(scale_a, 8, 1) + b * pltpu.roll(scale_b, 8, 1)
    stats = jnp.where(lane < 8, top, total)
    ahead = pltpu.roll(stats, 124, 1)
    first = jnp.where(lane < 4, stats, ahead)
    second = jnp.where(lane < 4, ahead, pltpu.roll(stats, 120, 1))
    out_ref[:, SPAN:] = split_terms(fold(first, second), 8)

    def joined(head):
        cols = head_cols(head)
        return (
            a_ref[:, cols].astype(F32) * scale_a[:, head : head + 1]
            + b_ref[:, cols].astype(F32) * scale_b[:, head : head + 1]
        )

    for head in range(HEADS // 2):
        out_ref[:, head_cols(head)] = fold(joined(head), joined(head + HEADS // 2)).astype(BF16)


def finish_body(in_ref, comp_ref, row_ref):
    stats = join_terms(in_ref[:, SPAN:], 8).reshape(32, 8, 128)
    top = jnp.max(stats, 0)
    scale = jnp.exp2(stats - top[None])
    total = jnp.sum(stats * pltpu.roll(scale, 4, 2), 0)
    parts = []
    for head in range(HEADS // 2):
        data = in_ref[:, head_cols(head)].astype(F32).reshape(32, 8, 128)
        part = jnp.sum(data * scale[:, :, head : head + 1], 0)
        parts.append(part / total[:, head + 4 : head + 5])
    pooled = jnp.concatenate(parts, 1)
    power = jnp.broadcast_to(jnp.sum(pooled * pooled, 1, keepdims=True), (8, 128))
    power = power + pltpu.roll(power, 4, 0)
    scale = lax.rsqrt(power * (1.0 / WIDTH) + 1e-06)
    summary = (pooled * scale[:, :1]).astype(BF16)
    context = dot(summary, comp_ref[:SPAN]) + pltpu.roll(dot(summary, comp_ref[SPAN:]), 4, 0)
    row_ref[...] = context.astype(BF16).astype(F32)


def rank_body(row_ref, down_ref, rank_ref):
    context = row_ref[...].astype(BF16)
    rank = jnp.zeros((1, 128), F32)
    for seed in range(4):
        rank = rank + dot(context, down_ref[seed * 512 : (seed + 1) * 512, :])[seed : seed + 1]
    rank_ref[...] = jnp.broadcast_to(rank, (8, 128))


def cross_body(row_ref, a_ref, b_ref, c_ref, d_ref, up_ref, bias_ref, out_ref):
    rank = a_ref[0:1] + b_ref[0:1] + c_ref[0:1] + d_ref[0:1]
    rank = jnp.broadcast_to(rank, (8, 128)).astype(BF16)
    lifted = dot(rank, up_ref[...])[0:1]
    base = jnp.concatenate([row_ref[seed : seed + 1, :] for seed in range(4)], 1)
    out_ref[...] = base * (lifted + bias_ref[...].astype(F32)) + base


def shape(dims, dtype):
    return jax.ShapeDtypeStruct(dims, dtype)


VMEM = pl.BlockSpec(memory_space=pltpu.VMEM)
SMEM = pl.BlockSpec(memory_space=pltpu.SMEM)
HBM = pl.BlockSpec(memory_space=pltpu.HBM)


def call(name, body, outs, args, ins=None, scratch=(), out_specs=None, flops=1 << 28, nbytes=1 << 20, limit=16):
    return pl.pallas_call(
        body,
        in_specs=ins or [VMEM] * len(args),
        out_specs=out_specs or [VMEM] * len(outs),
        out_shape=outs,
        scratch_shapes=list(scratch),
        compiler_params=pltpu.CompilerParams(vmem_limit_bytes=limit << 20),
        cost_estimate=pl.CostEstimate(flops=1, bytes_accessed=1, transcendentals=0),
        name=name,
    )(*args)


def in_hbm(array):
    return pltpu.with_memory_space_constraint(array, pltpu.HBM)


def after(values, result):
    return lax.optimization_barrier((values, result))


def swap(value):
    return lax.ppermute(value, ("y", "x"), [(q * 4 + g, g * 4 + q) for q in range(4) for g in range(4)])


def turn(value, by):
    return lax.ppermute(value, "x", [(i, (i + by) % 4) for i in range(4)])


def first_rows(value):
    pairs = [
        (((x * 8 + z) * 4) + y, ((y * 8 + (z ^ (2 * y))) * 4) + x)
        for x in range(4) for y in range(4) for z in range(8)
    ]
    return lax.ppermute(value, ("y", "z", "x"), pairs)


def flip(value, axis, size, bit):
    return lax.ppermute(value, axis, [(i, i ^ bit) for i in range(size)])


def local(
    events, segment_ids, event_mask, nonseq, seed_tokens, w_query, w_key, w_value, w_out, w_pers,
    w_comp, w_down, w_up, cross_bias,
):
    x = events[0]
    first = (lax.axis_index("y") == 0) & (lax.axis_index("z") == 0) & (lax.axis_index("core") == 0)
    core = lax.axis_index("core").astype(jnp.int32)
    own_user = (lax.axis_index("z") ^ (2 * lax.axis_index("y"))).astype(jnp.int32) * 2 + core
    place = jnp.stack([core, own_user, first.astype(jnp.int32)])
    line = ("y", "z", "core")
    onward = [(i, i + 1) for i in range(63)]
    square_w = shape((WIDTH, WIDTH), BF16)
    rows_b = shape((ROWS, WIDTH), BF16)
    rows_f = shape((ROWS, WIDTH), F32)
    half_f = shape((HALF, WIDTH), F32)
    half_b = shape((HALF, WIDTH), BF16)
    line_i = shape((1, ROWS), jnp.int32)

    users = [first_rows(nonseq)]
    carried = shape((HALF + 16, WIDTH), BF16)
    high_x, low_x, segs, flags = call(
        "load", load_body, [carried, half_b] + [line_i] * 2, [in_hbm(a) for a in (x, segment_ids, event_mask)],
        [HBM] * 3, [pltpu.SemaphoreType.DMA((6,))],
    )
    near_x = lax.ppermute(high_x, line, onward)
    far_x = lax.ppermute(low_x, line, onward)

    w_query, w_key, w_value, w_out, q, k, v, bias = call(
        "project", project_body,
        [square_w] * 4 + [rows_b] * 3 + [shape((ROWS, ROWS), F32)],
        [place, low_x, high_x] + [in_hbm(a) for a in (w_query, w_key, w_value, w_out)] + [segs, flags],
        [SMEM] + [VMEM] * 2 + [HBM] * 4 + [VMEM] * 2,
        [pltpu.SemaphoreType.DMA((1 + 3 * WIDTH // PIECE,))],
        flops=3 << 30, nbytes=8 << 20, limit=16,
    )
    users, q = after(users, q)
    users.append(flip(users[0], "core", 2, 1))
    users.append(flip(jnp.concatenate(users, 0), "z", 8, 1))
    acc, top, total = call(
        "own", own_body, [rows_f] * 3, [q, k, v, bias], flops=2 << 30, nbytes=4 << 20, limit=16
    )
    users, acc = after(users, acc)
    users.append(flip(jnp.concatenate(users, 0), "y", 4, 2))

    scratch = [
        pltpu.VMEM((ROWS, HALF), F32), pltpu.VMEM((HALF, WIDTH), BF16), pltpu.VMEM((HALF, WIDTH), BF16),
        pltpu.VMEM((HALF, WIDTH), BF16),
    ]
    high, hid_high, acc, top, total = call(
        "near", near_body, [half_f, half_b] + [half_f] * 3,
        [place, near_x, w_key, w_value, w_out, high_x, q, acc, top, total, segs],
        [SMEM] + [VMEM] * 10, scratch, flops=3 << 30, nbytes=6 << 20,
    )
    users, top = after(users, top)
    users.append(flip(jnp.concatenate(users, 0), "y", 4, 1))
    low, hid_low = call(
        "far", far_body, [half_f, half_b],
        [place, far_x, w_key, w_value, w_out, low_x, q, acc, top, total, segs, near_x],
        [SMEM] + [VMEM] * 11, [pltpu.VMEM((HALF, HALF), F32)] + scratch[1:],
        flops=2 << 30, nbytes=4 << 20,
    )
    few = shape((SEEDS, WIDTH), BF16)
    seed_query, user_query = call("query", query_body, [few, few], users + [w_pers, w_query, seed_tokens])
    part = shape((128, MESSAGE), BF16)
    keep, send, out = call(
        "pool", pool_body, [part, part, rows_f],
        [place, low, high, hid_low, hid_high, k, seed_query, user_query, segs, near_x, flags],
        [SMEM] + [VMEM] * 10, [pltpu.SemaphoreType.DMA((2,))], [VMEM, VMEM, HBM],
        flops=1 << 30, nbytes=3 << 20,
    )
    merged = call(
        "merge", merge_body, [shape((256, SPAN + EXTRA), BF16)], [keep, flip(send, "core", 2, 1)]
    )[0]
    pieces = lax.all_to_all(merged.reshape(32, 8, SPAN + EXTRA), ("y", "z"), 0, 0, tiled=True)
    row = call(
        "finish", finish_body, [shape((8, 512), F32)], [pieces.reshape(256, SPAN + EXTRA), w_comp]
    )[0]
    row = swap(row)
    rank = call("rank", rank_body, [shape((8, 128), F32)], [row, w_down])[0]
    ranks = [rank] + [turn(rank, by) for by in (1, 2, 3)]
    cross = call("cross", cross_body, [shape((1, 2048), F32)], [row] + ranks + [w_up, cross_bias[None]])[0]
    return out[None], cross


def solution(mesh):
    split = Mesh(mesh.devices.reshape(4, 8, 2, 4), ("y", "z", "core", "x"))
    seq = ("y", "z", "core")
    return jax.shard_map(
        local,
        mesh=split,
        in_specs=(
            P("x", seq, None), P("x", seq), P("x", seq), P(seq, None),
            P(), P(), P(), P(), P(), P(), P(),
            P("x", None), P(None, "x"), P("x"),
        ),
        out_specs=(P("x", seq, None), P(seq, "x")),
        check_vma=False,
    )
```

time: 143 us -> 87.7 us (0.61)
  the two profiles are of different devices: /device:TPU:38 before, /device:TPU:24 now
where the time goes in v2:
time: 87.7 us; the launch traced here: 87.4 us
  starting transfers between devices  28.9 us (33%)
  Pallas kernels  24.6 us (28%)
  blocking collectives  19.7 us (22%)
  waiting for transfers between devices  13.2 us (15%)
    pallas_call x11, Pallas kernels, call(): pl.pallas_call(body, in_specs=ins or [VMEM] * len(args), out_specs=out_sp...  24.6 us
    all_to_all x1, blocking collectives, local(): lax.all_to_all(merged.reshape(32, 8, SPAN + EXTRA), ('y', 'z'), 0, 0, til...  19.7 us
    ppermute x5, starting transfers between devices, flip(): return lax.ppermute(value, axis, [(i, i ^ bit) for i in range(size)])  8.07 us
    ppermute x1, starting transfers between devices, swap(): lax.ppermute(value, ('y', 'x'), [(q * 4 + g, g * 4 + q) for q in range(4)...  5.42 us
    ppermute x3, starting transfers between devices, turn(): return lax.ppermute(value, 'x', [(i, (i + by) % 4) for i in range(4)])  5.21 us
    ppermute x3, waiting for transfers between devices, turn(): return lax.ppermute(value, 'x', [(i, (i + by) % 4) for i in range(4)])  4.79 us
    ppermute x1, starting transfers between devices, first_rows(): return lax.ppermute(value, ('y', 'z', 'x'), pairs)  4.36 us
    ppermute x1, starting transfers between devices, local(): far_x = lax.ppermute(low_x, line, onward)  3.93 us
  transfers between devices with their start and end apart: 12, of which 8 were waited for; matrix products, arithmetic and copies ran while one was open for 0% of the time, Pallas kernels for 20%

profile of v2, /device:TPU:24, one launch (start us, length us, event | category | flops | bytes accessed | tf_op | source)
XLA Modules:
  0.0 87.4 jit_solution(12361391927161961453)
XLA Ops:
  0.6 1.3 %load.1 = (bf16[272,1024]{1,0:T(8,128)(2,1)S(1)}, bf16[256,1024]{1,0:T(8,128)(2,1)S(1)}, s32[1,512]{1,0:T(1,128)S(1)}, s32[1,512]{1,0:T(1,128)S(1)}) custom-call(bf16[512,1024]{1,0:T(8,128)(2,1)} %bitcast.9, s32[1,512]{1,0:T(1,128)} %seg_hbm.1, s32[1,512]{1,0:T(1,128)} %flag_hbm.1), custom_call_target="tpu_custom_call" | custom-call | flops 1 | bytes 1 | tf_op jit(solution)/shard_map/load/pallas_call | solution.py:363
  1.9 1.9 %collective-permute-start.2 = (bf16[272,1024]{1,0:T(8,128)(2,1)S(1)}, bf16[272,1024]{1,0:T(8,128)(2,1)S(1)}, u32[]{:S(2)}, u32[]{:S(2)}) collective-permute-start(bf16[272,1024]{1,0:T(8,128)(2,1)S(1)} %get-tuple-element.41.high_ref.x_ref), channel_id=1, source_target_pairs={{0,4},{4,8},{8,12},{12,16},{16,20},{20,24},{24,28},{28,32},{32,36}... | collective-permute-start | bytes 1671176 | tf_op jit(solution)/shard_map/ppermute | solution.py:427
  3.8 3.9 %collective-permute-start = (bf16[256,1024]{1,0:T(8,128)(2,1)S(1)}, bf16[256,1024]{1,0:T(8,128)(2,1)S(1)}, u32[]{:S(2)}, u32[]{:S(2)}) collective-permute-start(bf16[256,1024]{1,0:T(8,128)(2,1)S(1)} %get-tuple-element.40.low_ref.x_ref), channel_id=1, source_target_pairs={{0,4},{4,8},{8,12},{12,16},{16,20},{20,24},{24,28},{28,32},{32,36}... | collective-permute-start | bytes 1572872 | tf_op jit(solution)/shard_map/ppermute | solution.py:428
  7.8 4.4 %collective-permute-start.1 = (bf16[1,512]{1,0:T(2,128)(2,1)}, bf16[1,512]{1,0:T(2,128)(2,1)S(1)}, u32[]{:S(2)}, u32[]{:S(2)}) collective-permute-start(bf16[1,512]{1,0:T(2,128)(2,1)} %param.17), channel_id=1, source_target_pairs={{0,0},{8,8},{16,16},{24,24},{32,32},{40,40},{48,48},{56,56},{1,80}... | collective-permute-start | bytes 3080 | tf_op jit(solution)/shard_map/ppermute | solution.py:396
  12.2 6.2 %project.1 = (bf16[1024,1024]{1,0:T(8,128)(2,1)S(1)}, bf16[1024,1024]{1,0:T(8,128)(2,1)S(1)}, bf16[1024,1024]{1,0:T(8,128)(2,1)S(1)}, bf16[1024,1024]{1,0:T(8,12...) custom-call(s32[3]{0:T(128)S(1)} %pad_add_fusion.place_ref, ...), custom_call_target="tpu_custom_call" | custom-call | flops 1 | bytes 1 | tf_op jit(solution)/shard_map/project/pallas_call | solution.py:363
  18.4 1.5 %collective-permute-done.1.a_ref = bf16[1,512]{1,0:T(2,128)(2,1)S(1)} collective-permute-done((bf16[1,512]{1,0:T(2,128)(2,1)}, bf16[1,512]{1,0:T(2,128)(2,1)S(1)}, u32[]{:S(2)}, u32[]{:S(2)}) %collective-permute-start.1) | collective-permute-done | bytes 1056 | tf_op jit(solution)/shard_map/ppermute | solution.py:396
  19.9 5.5 %collective-permute-start.3 = (bf16[1,512]{1,0:T(2,128)(2,1)S(1)}, bf16[1,512]{1,0:T(2,128)(2,1)S(1)}, u32[]{:S(2)}, u32[]{:S(2)}) collective-permute-start(bf16[1,512]{1,0:T(2,128)(2,1)S(1)} %collective-permute-done.1.a_ref), channel_id=1, source_target_pairs={{0,4},{4,0},{1,5},{5,1},{2,6},{6,2},{3,7},{7,3},{8,12},{12,8},{9,1... | collective-permute-start | bytes 3080 | tf_op jit(solution)/shard_map/ppermute | solution.py:400
  25.4 0.8 collective-permute-done.3.b_ref
  26.3 3.3 %own.1 = (f32[512,1024]{1,0:T(8,128)S(1)}, f32[512,1024]{1,0:T(8,128)S(1)}, f32[512,1024]{1,0:T(8,128)S(1)}) custom-call(bf16[512,1024]{1,0:T(8,128)(2,1)S(1)} %get-tuple-element.48.q_ref, bf16[512,1024]{1,0:T(8,128)(2,1)S(1)} %get-tuple-element.50.k_ref, bf16[512,1024]{1,0:T(8,128)(2,1)S(1)} %get-tuple-element.51.v_ref, ...), custom_call_target="tpu_custom_call" | custom-call | flops 1 | bytes 1 | tf_op jit(solution)/shard_map/own/pallas_call | solution.py:363
  30.0 4.3 %near.1 = (f32[256,1024]{1,0:T(8,128)S(1)}, bf16[256,1024]{1,0:T(8,128)(2,1)S(1)}, f32[256,1024]{1,0:T(8,128)S(1)}, f32[256,1024]{1,0:T(8,128)S(1)}, f32[256,1024]{1,0:T(8,128)S(1)}) custom-call(s32[3]{0:T(128)S(1)} %pad_add_fusion.place_ref, bf16[272,1024]{1,0:T(8,128)(2,1)S(1)} %collective-permute-done.2.xp_ref.marks_ref, ...), custom_call_target="tpu_custom_call" | custom-call | flops 1 | bytes 1 | tf_op jit(solution)/shard_map/near/pallas_call | solution.py:363
  34.3 0.8 collective-permute-done.5.d_ref
  35.1 2.3 %collective-permute-start.6 = (bf16[8,512]{1,0:T(8,128)(2,1)S(1)}, bf16[8,512]{1,0:T(8,128)(2,1)S(1)}, u32[]{:S(2)}, u32[]{:S(2)}) collective-permute-start(bf16[8,512]{1,0:T(8,128)(2,1)S(1)} %pad_maximum_fusion), channel_id=1, source_target_pairs={{0,64},{64,0},{128,192},{192,128},{1,65},{65,1},{129,193},{193,129... | collective-permute-start | bytes 24584 | tf_op jit(solution)/shard_map/ppermute | solution.py:400
  37.4 3.5 %far.1 = (f32[256,1024]{1,0:T(8,128)S(1)}, bf16[256,1024]{1,0:T(8,128)(2,1)S(1)}) custom-call(s32[3]{0:T(128)S(1)} %pad_add_fusion.place_ref, bf16[256,1024]{1,0:T(8,128)(2,1)S(1)} %collective-permute-done.xp_ref, bf16[1024,1024]{1,0:T(8,128)(2,1)S(1)} %get-tuple-element.44.wk_ref, bf16[1024,1024]{1,0:T(8,128)(2,1)S(1)} %get-tuple-element.45.wv_ref, ...), custom_call_target="tpu_custom_call" | custom-call | flops 1 | bytes 1 | tf_op jit(solution)/shard_map/far/pallas_call | solution.py:363
  41.6 3.1 %pool.1 = (bf16[128,1152]{1,0:T(8,128)(2,1)S(1)}, bf16[128,1152]{1,0:T(8,128)(2,1)S(1)}, f32[512,1024]{1,0:T(8,128)}) custom-call(s32[3]{0:T(128)S(1)} %pad_add_fusion.place_ref, f32[256,1024]{1,0:T(8,128)S(1)} %get-tuple-element.64.low_ref, f32[256,1024]{1,0:T(8,128)S(1)} %get-tuple-element.65.high_ref, ...), custom_call_target="tpu_custom_call" | custom-call | flops 1 | bytes 1 | tf_op jit(solution)/shard_map/pool/pallas_call | solution.py:363
  44.8 1.6 %collective-permute-done.7.b_ref = bf16[128,1152]{1,0:T(8,128)(2,1)S(1)} collective-permute-done((bf16[128,1152]{1,0:T(8,128)(2,1)S(1)}, bf16[128,1152]{1,0:T(8,128)(2,1)S(1)}, u32[]{:S(2)}, u32[]{:S(2)}) %collective-permute-start.7) | collective-permute-done | bytes 294944 | tf_op jit(solution)/shard_map/ppermute | solution.py:400
  46.3 0.6 merge.1
  47.0 19.7 %all_to_all.5 = bf16[32,8,640]{2,1,0:T(8,128)(2,1)S(1)} all-to-all(bf16[32,8,640]{2,1,0:T(8,128)(2,1)S(1)} %bitcast.7), channel_id=1, replica_groups=mesh['y'=4,'z'=8,'core'=2,'x'=4] {'y','z'}, dimensions={0} | all-to-all | bytes 655360 | tf_op jit(solution)/shard_map/all_to_all | solution.py:476
  66.7 0.8 finish.1
  67.5 5.4 %collective-permute-start.8 = (f32[8,512]{1,0:T(8,128)S(1)}, f32[8,512]{1,0:T(8,128)S(1)}, u32[]{:S(2)}, u32[]{:S(2)}) collective-permute-start(f32[8,512]{1,0:T(8,128)S(1)} %finish.1), channel_id=1, source_target_pairs={{0,0},{1,64},{2,128},{3,192},{64,1},{65,65},{66,129},{67,193},{128... | collective-permute-start | bytes 49160 | tf_op jit(solution)/shard_map/ppermute | solution.py:384
  72.9 3.5 %collective-permute-done.8.row_ref = f32[8,512]{1,0:T(8,128)S(1)} collective-permute-done((f32[8,512]{1,0:T(8,128)S(1)}, f32[8,512]{1,0:T(8,128)S(1)}, u32[]{:S(2)}, u32[]{:S(2)}) %collective-permute-start.8) | collective-permute-done | bytes 16416 | tf_op jit(solution)/shard_map/ppermute | solution.py:384
  76.7 5.1 %collective-permute-start.11 = (f32[8,128]{1,0:T(8,128)S(1)}, f32[8,128]{1,0:T(8,128)S(1)}, u32[]{:S(2)}, u32[]{:S(2)}) collective-permute-start(f32[8,128]{1,0:T(8,128)S(1)} %rank.1.a_ref), channel_id=1, source_target_pairs={{0,3},{1,0},{2,1},{3,2},{4,7},{5,4},{6,5},{7,6},{8,11},{9,8},{10,9... | collective-permute-start | bytes 12296 | tf_op jit(solution)/shard_map/ppermute | solution.py:388
  81.9 1.3 %collective-permute-done.11.d_ref = f32[8,128]{1,0:T(8,128)S(1)} collective-permute-done((f32[8,128]{1,0:T(8,128)S(1)}, f32[8,128]{1,0:T(8,128)S(1)}, u32[]{:S(2)}, u32[]{:S(2)}) %collective-permute-start.11) | collective-permute-done | bytes 4128 | tf_op jit(solution)/shard_map/ppermute | solution.py:388
  83.2 3.5 %collective-permute-done.9.b_ref = f32[8,128]{1,0:T(8,128)S(1)} collective-permute-done((f32[8,128]{1,0:T(8,128)S(1)}, f32[8,128]{1,0:T(8,128)S(1)}, u32[]{:S(2)}, u32[]{:S(2)}) %collective-permute-start.9) | collective-permute-done | bytes 4128 | tf_op jit(solution)/shard_map/ppermute | solution.py:388
  86.7 0.8 cross.1
  (29 shorter events, 1.5 us)
Async XLA Ops:
  1.9 28.1 %collective-permute-start.2 = (bf16[272,1024]{1,0:T(8,128)(2,1)S(1)}, bf16[272,1024]{1,0:T(8,128)(2,1)S(1)}, u32[]{:S(2)}, u32[]{:S(2)}) collective-permute-start(bf16[272,1024]{1,0:T(8,128)(2,1)S(1)} %get-tuple-element.41.high_ref.x_ref), channel_id=1, source_target_pairs={{0,4},{4,8},{8,12},{12,16},{16,20},{20,24},{24,28},{28,32},{32,36}... | collective-permute-start | bytes 1671176 | tf_op jit(solution)/shard_map/ppermute | solution.py:427
  3.8 33.6 %collective-permute-start = (bf16[256,1024]{1,0:T(8,128)(2,1)S(1)}, bf16[256,1024]{1,0:T(8,128)(2,1)S(1)}, u32[]{:S(2)}, u32[]{:S(2)}) collective-permute-start(bf16[256,1024]{1,0:T(8,128)(2,1)S(1)} %get-tuple-element.40.low_ref.x_ref), channel_id=1, source_target_pairs={{0,4},{4,8},{8,12},{12,16},{16,20},{20,24},{24,28},{28,32},{32,36}... | collective-permute-start | bytes 1572872 | tf_op jit(solution)/shard_map/ppermute | solution.py:428
  7.8 12.1 %collective-permute-start.1 = (bf16[1,512]{1,0:T(2,128)(2,1)}, bf16[1,512]{1,0:T(2,128)(2,1)S(1)}, u32[]{:S(2)}, u32[]{:S(2)}) collective-permute-start(bf16[1,512]{1,0:T(2,128)(2,1)} %param.17), channel_id=1, source_target_pairs={{0,0},{8,8},{16,16},{24,24},{32,32},{40,40},{48,48},{56,56},{1,80}... | collective-permute-start | bytes 3080 | tf_op jit(solution)/shard_map/ppermute | solution.py:396
  19.9 6.3 %collective-permute-start.3 = (bf16[1,512]{1,0:T(2,128)(2,1)S(1)}, bf16[1,512]{1,0:T(2,128)(2,1)S(1)}, u32[]{:S(2)}, u32[]{:S(2)}) collective-permute-start(bf16[1,512]{1,0:T(2,128)(2,1)S(1)} %collective-permute-done.1.a_ref), channel_id=1, source_target_pairs={{0,4},{4,0},{1,5},{5,1},{2,6},{6,2},{3,7},{7,3},{8,12},{12,8},{9,1... | collective-permute-start | bytes 3080 | tf_op jit(solution)/shard_map/ppermute | solution.py:400
  26.2 3.7 %collective-permute-start.4 = (bf16[2,512]{1,0:T(2,128)(2,1)S(1)}, bf16[2,512]{1,0:T(2,128)(2,1)S(1)}, u32[]{:S(2)}, u32[]{:S(2)}) collective-permute-start(bf16[2,512]{1,0:T(2,128)(2,1)S(1)} %pad_maximum_fusion.2), channel_id=1, source_target_pairs={{0,8},{8,0},{16,24},{24,16},{32,40},{40,32},{48,56},{56,48},{1,9},... | collective-permute-start | bytes 6152 | tf_op jit(solution)/shard_map/ppermute | solution.py:400
  29.9 5.2 %collective-permute-start.5 = (bf16[4,512]{1,0:T(4,128)(2,1)S(1)}, bf16[4,512]{1,0:T(4,128)(2,1)S(1)}, u32[]{:S(2)}, u32[]{:S(2)}) collective-permute-start(bf16[4,512]{1,0:T(4,128)(2,1)S(1)} %pad_maximum_fusion.1), channel_id=1, source_target_pairs={{0,128},{64,192},{128,0},{192,64},{1,129},{65,193},{129,1},{193,65... | collective-permute-start | bytes 12296 | tf_op jit(solution)/shard_map/ppermute | solution.py:400
  35.1 5.8 %collective-permute-start.6 = (bf16[8,512]{1,0:T(8,128)(2,1)S(1)}, bf16[8,512]{1,0:T(8,128)(2,1)S(1)}, u32[]{:S(2)}, u32[]{:S(2)}) collective-permute-start(bf16[8,512]{1,0:T(8,128)(2,1)S(1)} %pad_maximum_fusion), channel_id=1, source_target_pairs={{0,64},{64,0},{128,192},{192,128},{1,65},{65,1},{129,193},{193,129... | collective-permute-start | bytes 24584 | tf_op jit(solution)/shard_map/ppermute | solution.py:400
  37.4 3.6 %copy-start.1 = (bf16[512,1024]{1,0:T(8,128)(2,1)S(1)}, bf16[512,1024]{1,0:T(8,128)(2,1)}, u32[]{:S(2)}) copy-start(bf16[512,1024]{1,0:T(8,128)(2,1)} %pers_ref.1) | copy-start | bytes 3145732
  37.4 3.6 %copy-start.4 = (bf16[16,1024]{1,0:T(8,128)(2,1)S(1)}, bf16[16,1024]{1,0:T(8,128)(2,1)}, u32[]{:S(2)}) copy-start(bf16[16,1024]{1,0:T(8,128)(2,1)} %seed_ref.1) | copy-start | bytes 98308
  41.6 25.1 %copy-start = (bf16[1024,512]{1,0:T(8,128)(2,1)S(1)}, bf16[1024,512]{1,0:T(8,128)(2,1)}, u32[]{:S(2)}) copy-start(bf16[1024,512]{1,0:T(8,128)(2,1)} %comp_ref.1) | copy-start | bytes 3145732
  44.6 31.8 %copy-start.2 = (bf16[2048,128]{1,0:T(8,128)(2,1)S(1)}, bf16[2048,128]{1,0:T(8,128)(2,1)}, u32[]{:S(2)}) copy-start(bf16[2048,128]{1,0:T(8,128)(2,1)} %down_ref.1) | copy-start | bytes 1572868
  44.7 37.2 %copy-start.5 = (bf16[2048]{0:T(1024)(128)(2,1)S(1)}, bf16[2048]{0:T(1024)(128)(2,1)}, u32[]{:S(2)}) copy-start(bf16[2048]{0:T(1024)(128)(2,1)} %param.27) | copy-start | bytes 12292
  44.7 42.0 %copy-start.3 = (bf16[128,2048]{1,0:T(8,128)(2,1)S(1)}, bf16[128,2048]{1,0:T(8,128)(2,1)}, u32[]{:S(2)}) copy-start(bf16[128,2048]{1,0:T(8,128)(2,1)} %up_ref.1) | copy-start | bytes 1572868
  44.7 1.7 %collective-permute-start.7 = (bf16[128,1152]{1,0:T(8,128)(2,1)S(1)}, bf16[128,1152]{1,0:T(8,128)(2,1)S(1)}, u32[]{:S(2)}, u32[]{:S(2)}) collective-permute-start(bf16[128,1152]{1,0:T(8,128)(2,1)S(1)} %get-tuple-element.77), channel_id=1, source_target_pairs={{0,4},{4,0},{1,5},{5,1},{2,6},{6,2},{3,7},{7,3},{8,12},{12,8},{9,1... | collective-permute-start | bytes 884744 | tf_op jit(solution)/shard_map/ppermute | solution.py:400
  67.5 8.9 %collective-permute-start.8 = (f32[8,512]{1,0:T(8,128)S(1)}, f32[8,512]{1,0:T(8,128)S(1)}, u32[]{:S(2)}, u32[]{:S(2)}) collective-permute-start(f32[8,512]{1,0:T(8,128)S(1)} %finish.1), channel_id=1, source_target_pairs={{0,0},{1,64},{2,128},{3,192},{64,1},{65,65},{66,129},{67,193},{128... | collective-permute-start | bytes 49160 | tf_op jit(solution)/shard_map/ppermute | solution.py:384
  76.6 5.2 %collective-permute-start.10 = (f32[8,128]{1,0:T(8,128)S(1)}, f32[8,128]{1,0:T(8,128)S(1)}, u32[]{:S(2)}, u32[]{:S(2)}) collective-permute-start(f32[8,128]{1,0:T(8,128)S(1)} %rank.1.a_ref), channel_id=1, source_target_pairs={{0,2},{1,3},{2,0},{3,1},{4,6},{5,7},{6,4},{7,5},{8,10},{9,11},{10,... | collective-permute-start | bytes 12296 | tf_op jit(solution)/shard_map/ppermute | solution.py:388
  76.7 6.5 %collective-permute-start.11 = (f32[8,128]{1,0:T(8,128)S(1)}, f32[8,128]{1,0:T(8,128)S(1)}, u32[]{:S(2)}, u32[]{:S(2)}) collective-permute-start(f32[8,128]{1,0:T(8,128)S(1)} %rank.1.a_ref), channel_id=1, source_target_pairs={{0,3},{1,0},{2,1},{3,2},{4,7},{5,4},{6,5},{7,6},{8,11},{9,8},{10,9... | collective-permute-start | bytes 12296 | tf_op jit(solution)/shard_map/ppermute | solution.py:388
  81.8 4.8 %collective-permute-start.9 = (f32[8,128]{1,0:T(8,128)S(1)}, f32[8,128]{1,0:T(8,128)S(1)}, u32[]{:S(2)}, u32[]{:S(2)}) collective-permute-start(f32[8,128]{1,0:T(8,128)S(1)} %rank.1.a_ref), channel_id=1, source_target_pairs={{0,1},{1,2},{2,3},{3,0},{4,5},{5,6},{6,7},{7,4},{8,9},{9,10},{10,1... | collective-permute-start | bytes 12296 | tf_op jit(solution)/shard_map/ppermute | solution.py:388

commit v3 on v2

--- a/solution.py
+++ b/solution.py
@@ -13,7 +13,6 @@
 ROWS = 512
 WIDTH = 1024
 HALF = 256
-CHUNK = 256
 PIECE = 512
 EXTRA = 128
 MESSAGE = WIDTH + EXTRA
@@ -58,58 +57,60 @@
     return jnp.concatenate([values, jnp.ones(values.shape, BF16)], 1)
 
 
-def load_body(x_hbm, seg_hbm, flag_hbm, high_ref, low_ref, seg_ref, flag_ref, sems):
-    quarter = HALF // 2
+def load_body(x_hbm, seg_hbm, flag_hbm, x_ref, seg_ref, flag_ref, sems):
+    quarter = ROWS // 4
     copies = [
         pltpu.make_async_copy(seg_hbm, seg_ref, sems.at[0]),
         pltpu.make_async_copy(flag_hbm, flag_ref, sems.at[1]),
     ]
-    for start, target in ((HALF, high_ref), (0, low_ref)):
-        for at in (0, quarter):
-            copies.append(
-                pltpu.make_async_copy(
-                    x_hbm.at[pl.ds(start + at, quarter)], target.at[pl.ds(at, quarter)], sems.at[len(copies)]
-                )
-            )
+    for at in range(0, ROWS, quarter):
+        rows = pl.ds(at, quarter)
+        copies.append(pltpu.make_async_copy(x_hbm.at[rows], x_ref.at[rows], sems.at[len(copies)]))
     for copy in copies:
         copy.start()
     copies[0].wait()
     copies[1].wait()
     row, _ = square(16, ROWS)
     marks = jnp.where(row == 0, seg_ref[...], jnp.where(row == 1, flag_ref[...], 0))
-    high_ref[HALF:, :ROWS] = marks.astype(F32).astype(BF16)
-    high_ref[HALF:, ROWS:] = jnp.zeros((16, WIDTH - ROWS), BF16)
+    x_ref[ROWS:, :ROWS] = marks.astype(F32).astype(BF16)
+    x_ref[ROWS:, ROWS:] = jnp.zeros((16, WIDTH - ROWS), BF16)
     for copy in copies[2:]:
         copy.wait()
 
 
-def project_body(
-    place_ref, low_ref, high_ref, wq_hbm, wk_hbm, wv_hbm, wo_hbm, seg_ref, flag_ref,
-    wq_ref, wk_ref, wv_ref, wo_ref, q_ref, k_ref, v_ref, bias_ref, sems,
-):
+def project_body(place_ref, x_ref, *refs):
+    count = len(refs) // 3
     copies = []
-    triples = [(wq_hbm, wq_ref, q_ref), (wk_hbm, wk_ref, k_ref), (wv_hbm, wv_ref, v_ref)]
-    for source, target, _ in triples:
+    for source, target in zip(refs[:count], refs[count : 2 * count]):
         for at in range(0, WIDTH, PIECE):
             cols = slice(at, at + PIECE)
             copies.append(
-                pltpu.make_async_copy(source.at[:, cols], target.at[:, cols], sems.at[len(copies)])
+                pltpu.make_async_copy(source.at[:, cols], target.at[:, cols], refs[-1].at[len(copies)])
             )
-    copies.append(pltpu.make_async_copy(wo_hbm, wo_ref, sems.at[len(copies)]))
-    for copy in copies:
+    ahead = 3
+    for copy in copies[:ahead]:
         copy.start()
-    row, col = square(ROWS, ROWS)
-    same = same_user(seg_ref[...], seg_ref[...], flag_ref[...])
-    bias_ref[...] = jnp.where((same & (col < row)) | (col == row), 0.0, NEGATIVE)
-    x = jnp.concatenate([low_ref[...], high_ref[:HALF]], 0)
+    x = x_ref[:ROWS]
     at = 0
-    for _, weight, result in triples:
+    for weight, result in zip(refs[count : 2 * count], refs[2 * count : 3 * count]):
         for start in range(0, WIDTH, PIECE):
             cols = slice(start, start + PIECE)
             copies[at].wait()
+            if at + ahead < len(copies):
+                copies[at + ahead].start()
             result[:, cols] = dot(x, weight[:, cols]).astype(BF16)
             at += 1
-    copies[at].wait()
+
+
+def project(place, x, *weights):
+    count = len(weights)
+    found = call(
+        "project", project_body,
+        [shape((WIDTH, WIDTH), BF16)] * count + [shape((ROWS, WIDTH), BF16)] * count,
+        [place, x] + [in_hbm(weight) for weight in weights], [SMEM, VMEM] + [HBM] * count,
+        [pltpu.SemaphoreType.DMA((count * WIDTH // PIECE,))],
+    )
+    return found[:count], found[count:]
 
 
 def query_body(a_ref, b_ref, c_ref, d_ref, e_ref, pers_ref, wq_ref, seed_ref, sq_ref, uq_ref):
@@ -121,91 +122,74 @@
     uq_ref[...] = queries[SEEDS:]
 
 
-def own_body(q_ref, k_ref, v_ref, bias_ref, acc_ref, top_ref, total_ref):
+def marks_of(place_ref, near_ref, cols):
+    marks = near_ref[ROWS:, cols].astype(F32).astype(jnp.int32)
+    return jnp.where(place_ref[2] == 1, -1, marks[0:1]), marks[1:2]
+
+
+def masked(segments, key_segments, key_flags, ahead):
+    count = key_segments.shape[1]
+    row, col = square(HALF, count)
+    row = row + ahead
+    same = same_user(segments, key_segments, key_flags)
+    inside = (col < row) & (col > row - ROWS)
+    return jnp.where((same & inside) | (col == row), 0.0, NEGATIVE)
+
+
+def attend(queries, keys, values, bias):
+    score = dot_rows(queries, keys) * SCALE + bias
+    top = jnp.max(score, 1, keepdims=True)
+    mixed = dot(jnp.exp2(score - top).astype(BF16), beside_ones(values))
+    return (mixed[:, :HEAD_DIM] / mixed[:, HEAD_DIM:]).astype(BF16)
+
+
+def near_body(
+    place_ref, xp_ref, wk_ref, wv_ref, wo_hbm, x_ref, q_ref, k_ref, v_ref, seg_ref, flag_ref,
+    out_ref, hid_ref, key_ref, value_ref, wo_ref, bias_ref, context_ref, sems,
+):
+    copy = pltpu.make_async_copy(wo_hbm, wo_ref, sems.at[0])
+    copy.start()
+    segp, flagp = marks_of(place_ref, xp_ref, slice(HALF, ROWS))
+    segments = jnp.concatenate([segp, seg_ref[...]], 1)
+    flags = jnp.concatenate([flagp, flag_ref[...]], 1)
+    bias_ref[...] = masked(seg_ref[:, HALF:], segments, flags, ROWS)
+    xp = xp_ref[HALF:ROWS]
+    key_ref[...] = dot(xp, wk_ref[...]).astype(BF16)
+    value_ref[...] = dot(xp, wv_ref[...]).astype(BF16)
     for head in range(HEADS):
         cols = head_cols(head)
-        values = beside_ones(v_ref[:, cols])
-        for at in range(0, ROWS, CHUNK):
-            end = at + CHUNK
-            score = dot_rows(q_ref[at:end, cols], k_ref[:end, cols]) * SCALE + bias_ref[at:end, :end]
-            top = jnp.max(score, 1, keepdims=True)
-            mixed = dot(jnp.exp2(score - top).astype(BF16), values[:end])
-            acc_ref[at:end, cols] = mixed[:, :HEAD_DIM]
-            total_ref[at:end, cols] = mixed[:, HEAD_DIM:]
-            top_ref[at:end, cols] = jnp.broadcast_to(top, (CHUNK, HEAD_DIM))
-
-
-def absorb(queries, keys, values, bias, mixed, top, total):
-    score = dot_rows(queries, keys) * SCALE + bias
-    before = top
-    top = jnp.maximum(before, jnp.max(score, 1, keepdims=True))
-    weights = [
-        jnp.exp2(score[:, at : at + HEAD_DIM] - top) for at in range(0, score.shape[1], HEAD_DIM)
-    ]
-    fresh = dot(jnp.concatenate(weights, 1).astype(BF16), values)
-    shrink = jnp.exp2(before - top)
-    return mixed * shrink + fresh[:, :HEAD_DIM], top, total * shrink + fresh[:, HEAD_DIM:]
-
-
-def marks_of(place_ref, near_ref, cols):
-    marks = near_ref[HALF:, cols].astype(F32).astype(jnp.int32)
-    return jnp.where(place_ref[2] == 1, -1, marks[0:1]), marks[1:2]
-
-
-def near_body(
-    place_ref, xp_ref, wk_ref, wv_ref, wo_ref, x_ref, q_ref, acc_ref, top_ref, total_ref, seg_ref,
-    out_ref, hid_ref, acc2_ref, top2_ref, total2_ref, bias_ref, key_ref, value_ref, context_ref,
+        context_ref[:, cols] = attend(
+            q_ref[HALF:, cols],
+            jnp.concatenate([key_ref[:, cols], k_ref[:, cols]], 0),
+            jnp.concatenate([value_ref[:, cols], v_ref[:, cols]], 0),
+            bias_ref[...],
+        )
+    copy.wait()
+    out = x_ref[HALF:ROWS].astype(F32) + dot(context_ref[...], wo_ref[...])
+    out_ref[...] = out
+    hid_ref[...] = out.astype(BF16)
+
+
+def far_body(
+    place_ref, xp_ref, wk_ref, wv_ref, wo_ref, x_ref, q_ref, k_ref, v_ref, keyp_ref, valuep_ref, seg_ref,
+    flag_ref, out_ref, hid_ref, key_ref, value_ref, bias_ref, context_ref,
 ):
-    segp, flagp = marks_of(place_ref, xp_ref, slice(HALF, ROWS))
-    row, col = square(ROWS, HALF)
-    same = same_user(seg_ref[...], segp, flagp)
-    bias_ref[...] = jnp.where(same & (col + HALF > row), 0.0, NEGATIVE)
+    segp, flagp = marks_of(place_ref, xp_ref, slice(0, ROWS))
+    segments = jnp.concatenate([segp, seg_ref[:, :HALF]], 1)
+    flags = jnp.concatenate([flagp, flag_ref[:, :HALF]], 1)
+    bias_ref[...] = masked(seg_ref[:, :HALF], segments, flags, ROWS)
     xp = xp_ref[:HALF]
     key_ref[...] = dot(xp, wk_ref[...]).astype(BF16)
     value_ref[...] = dot(xp, wv_ref[...]).astype(BF16)
     for head in range(HEADS):
         cols = head_cols(head)
-        values = beside_ones(value_ref[:, cols])
-        for at in range(0, ROWS, CHUNK):
-            end = at + CHUNK
-            first = max(at - HALF, 0)
-            mixed, top, total = absorb(
-                q_ref[at:end, cols], key_ref[first:, cols], values[first:], bias_ref[at:end, first:],
-                acc_ref[at:end, cols], top_ref[at:end, cols], total_ref[at:end, cols],
-            )
-            if at < HALF:
-                acc2_ref[at:end, cols] = mixed
-                top2_ref[at:end, cols] = top
-                total2_ref[at:end, cols] = total
-            else:
-                context_ref[at - HALF : end - HALF, cols] = (mixed / total).astype(BF16)
+        context_ref[:, cols] = attend(
+            q_ref[:HALF, cols],
+            jnp.concatenate([key_ref[:, cols], keyp_ref[:, cols], k_ref[:HALF, cols]], 0),
+            jnp.concatenate([value_ref[:, cols], valuep_ref[:, cols], v_ref[:HALF, cols]], 0),
+            bias_ref[...],
+        )
     out = x_ref[:HALF].astype(F32) + dot(context_ref[...], wo_ref[...])
-    out_ref[...] = out
-    hid_ref[...] = out.astype(BF16)
-
-
-def far_body(
-    place_ref, xp_ref, wk_ref, wv_ref, wo_ref, x_ref, q_ref, acc_ref, top_ref, total_ref, seg_ref, marks_ref,
-    out_ref, hid_ref, bias_ref, key_ref, value_ref, context_ref,
-):
-    segp, flagp = marks_of(place_ref, marks_ref, slice(0, HALF))
-    row, col = square(HALF, HALF)
-    same = same_user(seg_ref[:, :HALF], segp, flagp)
-    bias_ref[...] = jnp.where(same & (col > row), 0.0, NEGATIVE)
-    xp = xp_ref[...]
-    key_ref[...] = dot(xp, wk_ref[...]).astype(BF16)
-    value_ref[...] = dot(xp, wv_ref[...]).astype(BF16)
-    for head in range(HEADS):
-        cols = head_cols(head)
-        values = beside_ones(value_ref[:, cols])
-        for at in range(0, HALF, CHUNK):
-            end = at + CHUNK
-            mixed, top, total = absorb(
-                q_ref[at:end, cols], key_ref[at:, cols], values[at:], bias_ref[at:end, at:],
-                acc_ref[at:end, cols], top_ref[at:end, cols], total_ref[at:end, cols],
-            )
-            context_ref[at:end, cols] = (mixed / total).astype(BF16)
-    out = x_ref[...].astype(F32) + dot(context_ref[...], wo_ref[...])
     out_ref[...] = out
     hid_ref[...] = out.astype(BF16)
 
@@ -242,9 +226,7 @@
     user16 = ((row % 32) // 4) * 2 + (core ^ (row // 128))
     seed16 = ((row % 128) // 32) * 4 + row % 4
     pick_seed = jnp.where(col == seed16, 1.0, 0.0).astype(BF16)
-    apart = user16 ^ own_user
-    place = (apart & 3) | ((apart & 4) << 1) | ((apart & 8) >> 1)
-    pick_user = jnp.where(col == place, 1.0, 0.0).astype(BF16)
+    pick_user = jnp.where(col == (user16 ^ own_user), 1.0, 0.0).astype(BF16)
     seeds = dot(pick_seed, sq_ref[...]).astype(BF16)
     users = dot(pick_user, uq_ref[...]).astype(BF16)
 
@@ -388,14 +370,6 @@
     return lax.ppermute(value, "x", [(i, (i + by) % 4) for i in range(4)])
 
 
-def first_rows(value):
-    pairs = [
-        (((x * 8 + z) * 4) + y, ((y * 8 + (z ^ (2 * y))) * 4) + x)
-        for x in range(4) for y in range(4) for z in range(8)
-    ]
-    return lax.ppermute(value, ("y", "z", "x"), pairs)
-
-
 def flip(value, axis, size, bit):
     return lax.ppermute(value, axis, [(i, i ^ bit) for i in range(size)])
 
@@ -407,7 +381,7 @@
     x = events[0]
     first = (lax.axis_index("y") == 0) & (lax.axis_index("z") == 0) & (lax.axis_index("core") == 0)
     core = lax.axis_index("core").astype(jnp.int32)
-    own_user = (lax.axis_index("z") ^ (2 * lax.axis_index("y"))).astype(jnp.int32) * 2 + core
+    own_user = lax.axis_index("z").astype(jnp.int32) * 2 + core
     place = jnp.stack([core, own_user, first.astype(jnp.int32)])
     line = ("y", "z", "core")
     onward = [(i, i + 1) for i in range(63)]
@@ -418,55 +392,40 @@
     half_b = shape((HALF, WIDTH), BF16)
     line_i = shape((1, ROWS), jnp.int32)
 
-    users = [first_rows(nonseq)]
-    carried = shape((HALF + 16, WIDTH), BF16)
-    high_x, low_x, segs, flags = call(
-        "load", load_body, [carried, half_b] + [line_i] * 2, [in_hbm(a) for a in (x, segment_ids, event_mask)],
-        [HBM] * 3, [pltpu.SemaphoreType.DMA((6,))],
-    )
-    near_x = lax.ppermute(high_x, line, onward)
-    far_x = lax.ppermute(low_x, line, onward)
-
-    w_query, w_key, w_value, w_out, q, k, v, bias = call(
-        "project", project_body,
-        [square_w] * 4 + [rows_b] * 3 + [shape((ROWS, ROWS), F32)],
-        [place, low_x, high_x] + [in_hbm(a) for a in (w_query, w_key, w_value, w_out)] + [segs, flags],
-        [SMEM] + [VMEM] * 2 + [HBM] * 4 + [VMEM] * 2,
-        [pltpu.SemaphoreType.DMA((1 + 3 * WIDTH // PIECE,))],
-        flops=3 << 30, nbytes=8 << 20, limit=16,
-    )
+    users = [swap(nonseq)]
+    x, segs, flags = call(
+        "load", load_body, [shape((ROWS + 16, WIDTH), BF16)] + [line_i] * 2,
+        [in_hbm(a) for a in (x, segment_ids, event_mask)], [HBM] * 3, [pltpu.SemaphoreType.DMA((6,))],
+    )
+    prior = lax.ppermute(x, line, onward)
+
+    (w_query, w_key), (q, k) = project(place, x, w_query, w_key)
     users, q = after(users, q)
     users.append(flip(users[0], "core", 2, 1))
+    users, x = after(users, x)
     users.append(flip(jnp.concatenate(users, 0), "z", 8, 1))
-    acc, top, total = call(
-        "own", own_body, [rows_f] * 3, [q, k, v, bias], flops=2 << 30, nbytes=4 << 20, limit=16
-    )
-    users, acc = after(users, acc)
-    users.append(flip(jnp.concatenate(users, 0), "y", 4, 2))
-
-    scratch = [
-        pltpu.VMEM((ROWS, HALF), F32), pltpu.VMEM((HALF, WIDTH), BF16), pltpu.VMEM((HALF, WIDTH), BF16),
-        pltpu.VMEM((HALF, WIDTH), BF16),
-    ]
-    high, hid_high, acc, top, total = call(
-        "near", near_body, [half_f, half_b] + [half_f] * 3,
-        [place, near_x, w_key, w_value, w_out, high_x, q, acc, top, total, segs],
-        [SMEM] + [VMEM] * 10, scratch, flops=3 << 30, nbytes=6 << 20,
-    )
-    users, top = after(users, top)
-    users.append(flip(jnp.concatenate(users, 0), "y", 4, 1))
+    (w_value,), (v,) = project(place, x, w_value)
+    users, v = after(users, v)
+    users.append(flip(jnp.concatenate(users, 0), "z", 8, 2))
+    scratch = [pltpu.VMEM((HALF, HALF + ROWS), F32), pltpu.VMEM((HALF, WIDTH), BF16)]
+    high, hid_high, near_k, near_v, w_out = call(
+        "near", near_body, [half_f] + [half_b] * 3 + [square_w],
+        [place, prior, w_key, w_value, in_hbm(w_out), x, q, k, v, segs, flags],
+        [SMEM] + [VMEM] * 3 + [HBM] + [VMEM] * 6, scratch + [pltpu.SemaphoreType.DMA((1,))],
+    )
+    users, near_k = after(users, near_k)
+    users.append(flip(jnp.concatenate(users, 0), "z", 8, 4))
     low, hid_low = call(
         "far", far_body, [half_f, half_b],
-        [place, far_x, w_key, w_value, w_out, low_x, q, acc, top, total, segs, near_x],
-        [SMEM] + [VMEM] * 11, [pltpu.VMEM((HALF, HALF), F32)] + scratch[1:],
-        flops=2 << 30, nbytes=4 << 20,
+        [place, prior, w_key, w_value, w_out, x, q, k, v, near_k, near_v, segs, flags],
+        [SMEM] + [VMEM] * 12, [pltpu.VMEM((HALF, WIDTH), BF16)] * 2 + scratch,
     )
     few = shape((SEEDS, WIDTH), BF16)
     seed_query, user_query = call("query", query_body, [few, few], users + [w_pers, w_query, seed_tokens])
     part = shape((128, MESSAGE), BF16)
     keep, send, out = call(
         "pool", pool_body, [part, part, rows_f],
-        [place, low, high, hid_low, hid_high, k, seed_query, user_query, segs, near_x, flags],
+        [place, low, high, hid_low, hid_high, k, seed_query, user_query, segs, prior, flags],
         [SMEM] + [VMEM] * 10, [pltpu.SemaphoreType.DMA((2,))], [VMEM, VMEM, HBM],
         flops=1 << 30, nbytes=3 << 20,
     )

time: 87.7 us -> 84.5 us (0.964)
  the two profiles are of different devices: /device:TPU:24 before, /device:TPU:38 now
where the time goes in v3:
time: 84.5 us; the launch traced here: 84.3 us
  Pallas kernels  25.6 us (30%)
  starting transfers between devices  24.3 us (29%)
  blocking collectives  20.9 us (25%)
  waiting for transfers between devices  12.5 us (15%)
    pallas_call x11, Pallas kernels, call(): pl.pallas_call(body, in_specs=ins or [VMEM] * len(args), out_specs=out_sp...  25.6 us
    all_to_all x1, blocking collectives, local(): lax.all_to_all(merged.reshape(32, 8, SPAN + EXTRA), ('y', 'z'), 0, 0, til...  20.9 us
    ppermute x5, starting transfers between devices, flip(): return lax.ppermute(value, axis, [(i, i ^ bit) for i in range(size)])  9.99 us
    ppermute x2, starting transfers between devices, swap(): lax.ppermute(value, ('y', 'x'), [(q * 4 + g, g * 4 + q) for q in range(4)...  9.08 us
    ppermute x3, waiting for transfers between devices, turn(): return lax.ppermute(value, 'x', [(i, (i + by) % 4) for i in range(4)])  5.09 us
    ppermute x2, waiting for transfers between devices, swap(): lax.ppermute(value, ('y', 'x'), [(q * 4 + g, g * 4 + q) for q in range(4)...  4.71 us
    ppermute x3, starting transfers between devices, turn(): return lax.ppermute(value, 'x', [(i, (i + by) % 4) for i in range(4)])  3.31 us
    ppermute x5, waiting for transfers between devices, flip(): return lax.ppermute(value, axis, [(i, i ^ bit) for i in range(size)])  2.65 us
  transfers between devices with their start and end apart: 11, of which 6 were waited for; matrix products, arithmetic and copies ran while one was open for 0% of the time, Pallas kernels for 22%

profile of v3, /device:TPU:38, one launch (start us, length us, event | category | flops | bytes accessed | tf_op | source)
XLA Modules:
  0.0 84.3 jit_solution(10122375299486868643)
XLA Ops:
  0.6 1.3 %load.1 = (bf16[528,1024]{1,0:T(8,128)(2,1)S(1)}, s32[1,512]{1,0:T(1,128)S(1)}, s32[1,512]{1,0:T(1,128)S(1)}) custom-call(bf16[512,1024]{1,0:T(8,128)(2,1)} %bitcast.9, s32[1,512]{1,0:T(1,128)} %seg_hbm.1, s32[1,512]{1,0:T(1,128)} %flag_hbm.1), custom_call_target="tpu_custom_call" | custom-call | flops 1 | bytes 1 | tf_op jit(solution)/shard_map/load/pallas_call | solution.py:345
  1.9 1.9 %collective-permute-start = (bf16[528,1024]{1,0:T(8,128)(2,1)S(1)}, bf16[528,1024]{1,0:T(8,128)(2,1)S(1)}, u32[]{:S(2)}, u32[]{:S(2)}) collective-permute-start(bf16[528,1024]{1,0:T(8,128)(2,1)S(1)} %get-tuple-element.41.x_ref), channel_id=1, source_target_pairs={{0,4},{4,8},{8,12},{12,16},{16,20},{20,24},{24,28},{28,32},{32,36}... | collective-permute-start | bytes 3244040 | tf_op jit(solution)/shard_map/ppermute | solution.py:400
  3.8 4.8 %collective-permute-start.1 = (bf16[1,512]{1,0:T(2,128)(2,1)}, bf16[1,512]{1,0:T(2,128)(2,1)S(1)}, u32[]{:S(2)}, u32[]{:S(2)}) collective-permute-start(bf16[1,512]{1,0:T(2,128)(2,1)} %param.17), channel_id=1, source_target_pairs={{0,0},{1,64},{2,128},{3,192},{64,1},{65,65},{66,129},{67,193},{128... | collective-permute-start | bytes 3080 | tf_op jit(solution)/shard_map/ppermute | solution.py:366
  8.8 4.7 %project.2 = (bf16[1024,1024]{1,0:T(8,128)(2,1)S(1)}, bf16[1024,1024]{1,0:T(8,128)(2,1)S(1)}, bf16[512,1024]{1,0:T(8,128)(2,1)S(1)}, bf16[512,1024]{1,0:T(8,128)(2,1)S(1)}) custom-call(s32[3]{0:T(128)S(1)} %pad_add_fusion.place_ref, bf16[528,1024]{1,0:T(8,128)(2,1)S(1)} %get-tuple-element.41.x_ref, bf16[1024,1024]{1,0:T(8,128)(2,1)} %refs_0_.2, ...), custom_call_target="tpu_custom_call" | custom-call | flops 1 | bytes 1 | tf_op jit(solution)/shard_map/project/pallas_call | solution.py:345
  13.5 1.8 %collective-permute-start.2 = (bf16[1,512]{1,0:T(2,128)(2,1)S(1)}, bf16[1,512]{1,0:T(2,128)(2,1)S(1)}, u32[]{:S(2)}, u32[]{:S(2)}) collective-permute-start(bf16[1,512]{1,0:T(2,128)(2,1)S(1)} %collective-permute-done.1.a_ref), channel_id=1, source_target_pairs={{0,4},{4,0},{1,5},{5,1},{2,6},{6,2},{3,7},{7,3},{8,12},{12,8},{9,1... | collective-permute-start | bytes 3080 | tf_op jit(solution)/shard_map/ppermute | solution.py:374
  15.3 0.8 collective-permute-done.2.b_ref
  16.3 3.2 %project.3 = (bf16[1024,1024]{1,0:T(8,128)(2,1)S(1)}, bf16[512,1024]{1,0:T(8,128)(2,1)S(1)}) custom-call(s32[3]{0:T(128)S(1)} %pad_add_fusion.place_ref, bf16[528,1024]{1,0:T(8,128)(2,1)S(1)} %get-tuple-element.41.x_ref, bf16[1024,1024]{1,0:T(8,128)(2,1)} %refs_0_.3), custom_call_target="tpu_custom_call" | custom-call | flops 1 | bytes 1 | tf_op jit(solution)/shard_map/project/pallas_call | solution.py:345
  19.8 4.6 %collective-permute-start.4 = (bf16[4,512]{1,0:T(4,128)(2,1)S(1)}, bf16[4,512]{1,0:T(4,128)(2,1)S(1)}, u32[]{:S(2)}, u32[]{:S(2)}) collective-permute-start(bf16[4,512]{1,0:T(4,128)(2,1)S(1)} %pad_maximum_fusion.1), channel_id=1, source_target_pairs={{0,16},{8,24},{16,0},{24,8},{32,48},{40,56},{48,32},{56,40},{1,17}... | collective-permute-start | bytes 12296 | tf_op jit(solution)/shard_map/ppermute | solution.py:374
  24.4 5.2 %near.1 = (f32[256,1024]{1,0:T(8,128)S(1)}, bf16[256,1024]{1,0:T(8,128)(2,1)S(1)}, bf16[256,1024]{1,0:T(8,128)(2,1)S(1)}, bf16[256,1024]{1,0:T(8,128)(2,1)S(1)}, bf16[1024,1024]{1,0:T(8,128)(2,1)S(1)}) custom-call(s32[3]{0:T(128)S(1)} %pad_add_fusion.place_ref, bf16[528,1024]{1,0:T(8,128)(2,1)S(1)} %collective-permute-done.xp_ref.marks_ref, ...), custom_call_target="tpu_custom_call" | custom-call | flops 1 | bytes 1 | tf_op jit(solution)/shard_map/near/pallas_call | solution.py:345
  29.7 3.3 %collective-permute-start.5 = (bf16[8,512]{1,0:T(8,128)(2,1)S(1)}, bf16[8,512]{1,0:T(8,128)(2,1)S(1)}, u32[]{:S(2)}, u32[]{:S(2)}) collective-permute-start(bf16[8,512]{1,0:T(8,128)(2,1)S(1)} %pad_maximum_fusion), channel_id=1, source_target_pairs={{0,32},{8,40},{16,48},{24,56},{32,0},{40,8},{48,16},{56,24},{1,33}... | collective-permute-start | bytes 24584 | tf_op jit(solution)/shard_map/ppermute | solution.py:374
  33.0 5.1 %far.1 = (f32[256,1024]{1,0:T(8,128)S(1)}, bf16[256,1024]{1,0:T(8,128)(2,1)S(1)}) custom-call(s32[3]{0:T(128)S(1)} %pad_add_fusion.place_ref, bf16[528,1024]{1,0:T(8,128)(2,1)S(1)} %collective-permute-done.xp_ref.marks_ref, bf16[1024,1024]{1,0:T(8,128)(2,1)S(1)} %get-tuple-element.38.wk_ref, bf16[1024,1024]{1,0:T(8,128)(2,1)S(1)} %get-tuple-element.42.wv_ref, ...), custom_call_target="tpu_custom_call" | custom-call | flops 1 | bytes 1 | tf_op jit(solution)/shard_map/far/pallas_call | solution.py:345
  38.1 0.6 query.1
  38.7 3.1 %pool.1 = (bf16[128,1152]{1,0:T(8,128)(2,1)S(1)}, bf16[128,1152]{1,0:T(8,128)(2,1)S(1)}, f32[512,1024]{1,0:T(8,128)}) custom-call(s32[3]{0:T(128)S(1)} %pad_add_fusion.place_ref, f32[256,1024]{1,0:T(8,128)S(1)} %get-tuple-element.58.low_ref, f32[256,1024]{1,0:T(8,128)S(1)} %get-tuple-element.59.high_ref, ...), custom_call_target="tpu_custom_call" | custom-call | flops 1 | bytes 1 | tf_op jit(solution)/shard_map/pool/pallas_call | solution.py:345
  42.0 1.6 %collective-permute-done.6.b_ref = bf16[128,1152]{1,0:T(8,128)(2,1)S(1)} collective-permute-done((bf16[128,1152]{1,0:T(8,128)(2,1)S(1)}, bf16[128,1152]{1,0:T(8,128)(2,1)S(1)}, u32[]{:S(2)}, u32[]{:S(2)}) %collective-permute-start.6) | collective-permute-done | bytes 294944 | tf_op jit(solution)/shard_map/ppermute | solution.py:374
  43.5 0.6 merge.1
  44.2 20.9 %all_to_all.5 = bf16[32,8,640]{2,1,0:T(8,128)(2,1)S(1)} all-to-all(bf16[32,8,640]{2,1,0:T(8,128)(2,1)S(1)} %bitcast.7), channel_id=1, replica_groups=mesh['y'=4,'z'=8,'core'=2,'x'=4] {'y','z'}, dimensions={0} | all-to-all | bytes 655360 | tf_op jit(solution)/shard_map/all_to_all | solution.py:435
  65.1 0.8 finish.1
  65.9 4.2 %collective-permute-start.7 = (f32[8,512]{1,0:T(8,128)S(1)}, f32[8,512]{1,0:T(8,128)S(1)}, u32[]{:S(2)}, u32[]{:S(2)}) collective-permute-start(f32[8,512]{1,0:T(8,128)S(1)} %finish.1), channel_id=1, source_target_pairs={{0,0},{1,64},{2,128},{3,192},{64,1},{65,65},{66,129},{67,193},{128... | collective-permute-start | bytes 49160 | tf_op jit(solution)/shard_map/ppermute | solution.py:366
  70.2 4.7 %collective-permute-done.7.row_ref = f32[8,512]{1,0:T(8,128)S(1)} collective-permute-done((f32[8,512]{1,0:T(8,128)S(1)}, f32[8,512]{1,0:T(8,128)S(1)}, u32[]{:S(2)}, u32[]{:S(2)}) %collective-permute-start.7) | collective-permute-done | bytes 16416 | tf_op jit(solution)/shard_map/ppermute | solution.py:366
  75.1 1.1 %collective-permute-start.10 = (f32[8,128]{1,0:T(8,128)S(1)}, f32[8,128]{1,0:T(8,128)S(1)}, u32[]{:S(2)}, u32[]{:S(2)}) collective-permute-start(f32[8,128]{1,0:T(8,128)S(1)} %rank.1.a_ref), channel_id=1, source_target_pairs={{0,3},{1,0},{2,1},{3,2},{4,7},{5,4},{6,5},{7,6},{8,11},{9,8},{10,9... | collective-permute-start | bytes 12296 | tf_op jit(solution)/shard_map/ppermute | solution.py:370
  76.2 2.2 %collective-permute-start.8 = (f32[8,128]{1,0:T(8,128)S(1)}, f32[8,128]{1,0:T(8,128)S(1)}, u32[]{:S(2)}, u32[]{:S(2)}) collective-permute-start(f32[8,128]{1,0:T(8,128)S(1)} %rank.1.a_ref), channel_id=1, source_target_pairs={{0,1},{1,2},{2,3},{3,0},{4,5},{5,6},{6,7},{7,4},{8,9},{9,10},{10,1... | collective-permute-start | bytes 12296 | tf_op jit(solution)/shard_map/ppermute | solution.py:370
  78.4 1.6 %collective-permute-done.10.d_ref = f32[8,128]{1,0:T(8,128)S(1)} collective-permute-done((f32[8,128]{1,0:T(8,128)S(1)}, f32[8,128]{1,0:T(8,128)S(1)}, u32[]{:S(2)}, u32[]{:S(2)}) %collective-permute-start.10) | collective-permute-done | bytes 4128 | tf_op jit(solution)/shard_map/ppermute | solution.py:370
  79.9 3.5 %collective-permute-done.9.c_ref = f32[8,128]{1,0:T(8,128)S(1)} collective-permute-done((f32[8,128]{1,0:T(8,128)S(1)}, f32[8,128]{1,0:T(8,128)S(1)}, u32[]{:S(2)}, u32[]{:S(2)}) %collective-permute-start.9) | collective-permute-done | bytes 4128 | tf_op jit(solution)/shard_map/ppermute | solution.py:370
  83.5 0.8 cross.1
  (27 shorter events, 0.9 us)
Async XLA Ops:
  1.9 22.5 %collective-permute-start = (bf16[528,1024]{1,0:T(8,128)(2,1)S(1)}, bf16[528,1024]{1,0:T(8,128)(2,1)S(1)}, u32[]{:S(2)}, u32[]{:S(2)}) collective-permute-start(bf16[528,1024]{1,0:T(8,128)(2,1)S(1)} %get-tuple-element.41.x_ref), channel_id=1, source_target_pairs={{0,4},{4,8},{8,12},{12,16},{16,20},{20,24},{24,28},{28,32},{32,36}... | collective-permute-start | bytes 3244040 | tf_op jit(solution)/shard_map/ppermute | solution.py:400
  3.8 9.6 %collective-permute-start.1 = (bf16[1,512]{1,0:T(2,128)(2,1)}, bf16[1,512]{1,0:T(2,128)(2,1)S(1)}, u32[]{:S(2)}, u32[]{:S(2)}) collective-permute-start(bf16[1,512]{1,0:T(2,128)(2,1)} %param.17), channel_id=1, source_target_pairs={{0,0},{1,64},{2,128},{3,192},{64,1},{65,65},{66,129},{67,193},{128... | collective-permute-start | bytes 3080 | tf_op jit(solution)/shard_map/ppermute | solution.py:366
  13.5 2.7 %collective-permute-start.2 = (bf16[1,512]{1,0:T(2,128)(2,1)S(1)}, bf16[1,512]{1,0:T(2,128)(2,1)S(1)}, u32[]{:S(2)}, u32[]{:S(2)}) collective-permute-start(bf16[1,512]{1,0:T(2,128)(2,1)S(1)} %collective-permute-done.1.a_ref), channel_id=1, source_target_pairs={{0,4},{4,0},{1,5},{5,1},{2,6},{6,2},{3,7},{7,3},{8,12},{12,8},{9,1... | collective-permute-start | bytes 3080 | tf_op jit(solution)/shard_map/ppermute | solution.py:374
  16.1 3.7 %collective-permute-start.3 = (bf16[2,512]{1,0:T(2,128)(2,1)S(1)}, bf16[2,512]{1,0:T(2,128)(2,1)S(1)}, u32[]{:S(2)}, u32[]{:S(2)}) collective-permute-start(bf16[2,512]{1,0:T(2,128)(2,1)S(1)} %pad_maximum_fusion.2), channel_id=1, source_target_pairs={{0,8},{8,0},{16,24},{24,16},{32,40},{40,32},{48,56},{56,48},{1,9},... | collective-permute-start | bytes 6152 | tf_op jit(solution)/shard_map/ppermute | solution.py:374
  19.8 9.8 %collective-permute-start.4 = (bf16[4,512]{1,0:T(4,128)(2,1)S(1)}, bf16[4,512]{1,0:T(4,128)(2,1)S(1)}, u32[]{:S(2)}, u32[]{:S(2)}) collective-permute-start(bf16[4,512]{1,0:T(4,128)(2,1)S(1)} %pad_maximum_fusion.1), channel_id=1, source_target_pairs={{0,16},{8,24},{16,0},{24,8},{32,48},{40,56},{48,32},{56,40},{1,17}... | collective-permute-start | bytes 12296 | tf_op jit(solution)/shard_map/ppermute | solution.py:374
  29.7 8.4 %collective-permute-start.5 = (bf16[8,512]{1,0:T(8,128)(2,1)S(1)}, bf16[8,512]{1,0:T(8,128)(2,1)S(1)}, u32[]{:S(2)}, u32[]{:S(2)}) collective-permute-start(bf16[8,512]{1,0:T(8,128)(2,1)S(1)} %pad_maximum_fusion), channel_id=1, source_target_pairs={{0,32},{8,40},{16,48},{24,56},{32,0},{40,8},{48,16},{56,24},{1,33}... | collective-permute-start | bytes 24584 | tf_op jit(solution)/shard_map/ppermute | solution.py:374
  33.0 5.1 %copy-start.1 = (bf16[512,1024]{1,0:T(8,128)(2,1)S(1)}, bf16[512,1024]{1,0:T(8,128)(2,1)}, u32[]{:S(2)}) copy-start(bf16[512,1024]{1,0:T(8,128)(2,1)} %pers_ref.1) | copy-start | bytes 3145732
  33.0 5.1 %copy-start.4 = (bf16[16,1024]{1,0:T(8,128)(2,1)S(1)}, bf16[16,1024]{1,0:T(8,128)(2,1)}, u32[]{:S(2)}) copy-start(bf16[16,1024]{1,0:T(8,128)(2,1)} %seed_ref.1) | copy-start | bytes 98308
  41.8 23.3 %copy-start = (bf16[1024,512]{1,0:T(8,128)(2,1)S(1)}, bf16[1024,512]{1,0:T(8,128)(2,1)}, u32[]{:S(2)}) copy-start(bf16[1024,512]{1,0:T(8,128)(2,1)} %comp_ref.1) | copy-start | bytes 3145732
  41.8 33.1 %copy-start.2 = (bf16[2048,128]{1,0:T(8,128)(2,1)S(1)}, bf16[2048,128]{1,0:T(8,128)(2,1)}, u32[]{:S(2)}) copy-start(bf16[2048,128]{1,0:T(8,128)(2,1)} %down_ref.1) | copy-start | bytes 1572868
  41.8 36.5 %copy-start.5 = (bf16[2048]{0:T(1024)(128)(2,1)S(1)}, bf16[2048]{0:T(1024)(128)(2,1)}, u32[]{:S(2)}) copy-start(bf16[2048]{0:T(1024)(128)(2,1)} %param.27) | copy-start | bytes 12292
  41.8 41.6 %copy-start.3 = (bf16[128,2048]{1,0:T(8,128)(2,1)S(1)}, bf16[128,2048]{1,0:T(8,128)(2,1)}, u32[]{:S(2)}) copy-start(bf16[128,2048]{1,0:T(8,128)(2,1)} %up_ref.1) | copy-start | bytes 1572868
  41.8 1.7 %collective-permute-start.6 = (bf16[128,1152]{1,0:T(8,128)(2,1)S(1)}, bf16[128,1152]{1,0:T(8,128)(2,1)S(1)}, u32[]{:S(2)}, u32[]{:S(2)}) collective-permute-start(bf16[128,1152]{1,0:T(8,128)(2,1)S(1)} %get-tuple-element.71), channel_id=1, source_target_pairs={{0,4},{4,0},{1,5},{5,1},{2,6},{6,2},{3,7},{7,3},{8,12},{12,8},{9,1... | collective-permute-start | bytes 884744 | tf_op jit(solution)/shard_map/ppermute | solution.py:374
  65.9 8.9 %collective-permute-start.7 = (f32[8,512]{1,0:T(8,128)S(1)}, f32[8,512]{1,0:T(8,128)S(1)}, u32[]{:S(2)}, u32[]{:S(2)}) collective-permute-start(f32[8,512]{1,0:T(8,128)S(1)} %finish.1), channel_id=1, source_target_pairs={{0,0},{1,64},{2,128},{3,192},{64,1},{65,65},{66,129},{67,193},{128... | collective-permute-start | bytes 49160 | tf_op jit(solution)/shard_map/ppermute | solution.py:366
  75.1 4.9 %collective-permute-start.10 = (f32[8,128]{1,0:T(8,128)S(1)}, f32[8,128]{1,0:T(8,128)S(1)}, u32[]{:S(2)}, u32[]{:S(2)}) collective-permute-start(f32[8,128]{1,0:T(8,128)S(1)} %rank.1.a_ref), channel_id=1, source_target_pairs={{0,3},{1,0},{2,1},{3,2},{4,7},{5,4},{6,5},{7,6},{8,11},{9,8},{10,9... | collective-permute-start | bytes 12296 | tf_op jit(solution)/shard_map/ppermute | solution.py:370
  76.2 3.8 %collective-permute-start.8 = (f32[8,128]{1,0:T(8,128)S(1)}, f32[8,128]{1,0:T(8,128)S(1)}, u32[]{:S(2)}, u32[]{:S(2)}) collective-permute-start(f32[8,128]{1,0:T(8,128)S(1)} %rank.1.a_ref), channel_id=1, source_target_pairs={{0,1},{1,2},{2,3},{3,0},{4,5},{5,6},{6,7},{7,4},{8,9},{9,10},{10,1... | collective-permute-start | bytes 12296 | tf_op jit(solution)/shard_map/ppermute | solution.py:370
  78.4 5.1 %collective-permute-start.9 = (f32[8,128]{1,0:T(8,128)S(1)}, f32[8,128]{1,0:T(8,128)S(1)}, u32[]{:S(2)}, u32[]{:S(2)}) collective-permute-start(f32[8,128]{1,0:T(8,128)S(1)} %rank.1.a_ref), channel_id=1, source_target_pairs={{0,2},{1,3},{2,0},{3,1},{4,6},{5,7},{6,4},{7,5},{8,10},{9,11},{10,... | collective-permute-start | bytes 12296 | tf_op jit(solution)/shard_map/ppermute | solution.py:370

commit v4 on v3

--- a/solution.py
+++ b/solution.py
@@ -13,6 +13,7 @@
 ROWS = 512
 WIDTH = 1024
 HALF = 256
+CHUNK = 128
 PIECE = 512
 EXTRA = 128
 MESSAGE = WIDTH + EXTRA
@@ -158,12 +159,14 @@
     value_ref[...] = dot(xp, wv_ref[...]).astype(BF16)
     for head in range(HEADS):
         cols = head_cols(head)
-        context_ref[:, cols] = attend(
-            q_ref[HALF:, cols],
-            jnp.concatenate([key_ref[:, cols], k_ref[:, cols]], 0),
-            jnp.concatenate([value_ref[:, cols], v_ref[:, cols]], 0),
-            bias_ref[...],
-        )
+        keys = jnp.concatenate([key_ref[:, cols], k_ref[:, cols]], 0)
+        values = jnp.concatenate([value_ref[:, cols], v_ref[:, cols]], 0)
+        for at in range(0, HALF, CHUNK):
+            end = at + CHUNK
+            context_ref[at:end, cols] = attend(
+                q_ref[HALF + at : HALF + end, cols], keys[at : end + ROWS], values[at : end + ROWS],
+                bias_ref[at:end, at : end + ROWS],
+            )
     copy.wait()
     out = x_ref[HALF:ROWS].astype(F32) + dot(context_ref[...], wo_ref[...])
     out_ref[...] = out
@@ -183,12 +186,14 @@
     value_ref[...] = dot(xp, wv_ref[...]).astype(BF16)
     for head in range(HEADS):
         cols = head_cols(head)
-        context_ref[:, cols] = attend(
-            q_ref[:HALF, cols],
-            jnp.concatenate([key_ref[:, cols], keyp_ref[:, cols], k_ref[:HALF, cols]], 0),
-            jnp.concatenate([value_ref[:, cols], valuep_ref[:, cols], v_ref[:HALF, cols]], 0),
-            bias_ref[...],
-        )
+        keys = jnp.concatenate([key_ref[:, cols], keyp_ref[:, cols], k_ref[:HALF, cols]], 0)
+        values = jnp.concatenate([value_ref[:, cols], valuep_ref[:, cols], v_ref[:HALF, cols]], 0)
+        for at in range(0, HALF, CHUNK):
+            end = at + CHUNK
+            context_ref[at:end, cols] = attend(
+                q_ref[at : end, cols], keys[at : end + ROWS], values[at : end + ROWS],
+                bias_ref[at:end, at : end + ROWS],
+            )
     out = x_ref[:HALF].astype(F32) + dot(context_ref[...], wo_ref[...])
     out_ref[...] = out
     hid_ref[...] = out.astype(BF16)

time: 84.5 us -> 85.5 us (1.012)
  Pallas kernels: 25.6 us -> 26.5 us
    pallas_call x11, Pallas kernels: 25.6 us -> 26.5 us  [call(): pl.pallas_call(body, in_specs=ins or [VMEM] * len(args), out_specs=out_sp...]
where the time goes in v4:
time: 85.5 us; the launch traced here: 85.2 us
  Pallas kernels  26.5 us (31%)
  starting transfers between devices  24.3 us (28%)
  blocking collectives  20.9 us (24%)
  waiting for transfers between devices  12.5 us (15%)
    pallas_call x11, Pallas kernels, call(): pl.pallas_call(body, in_specs=ins or [VMEM] * len(args), out_specs=out_sp...  26.5 us
    all_to_all x1, blocking collectives, local(): lax.all_to_all(merged.reshape(32, 8, SPAN + EXTRA), ('y', 'z'), 0, 0, til...  20.9 us
    ppermute x5, starting transfers between devices, flip(): return lax.ppermute(value, axis, [(i, i ^ bit) for i in range(size)])  9.98 us
    ppermute x2, starting transfers between devices, swap(): lax.ppermute(value, ('y', 'x'), [(q * 4 + g, g * 4 + q) for q in range(4)...  9.07 us
    ppermute x3, waiting for transfers between devices, turn(): return lax.ppermute(value, 'x', [(i, (i + by) % 4) for i in range(4)])  5.09 us
    ppermute x2, waiting for transfers between devices, swap(): lax.ppermute(value, ('y', 'x'), [(q * 4 + g, g * 4 + q) for q in range(4)...  4.71 us
    ppermute x3, starting transfers between devices, turn(): return lax.ppermute(value, 'x', [(i, (i + by) % 4) for i in range(4)])  3.31 us
    ppermute x5, waiting for transfers between devices, flip(): return lax.ppermute(value, axis, [(i, i ^ bit) for i in range(size)])  2.65 us
  transfers between devices with their start and end apart: 11, of which 6 were waited for; matrix products, arithmetic and copies ran while one was open for 0% of the time, Pallas kernels for 22%

profile of v4, /device:TPU:38, one launch (start us, length us, event | category | flops | bytes accessed | tf_op | source)
XLA Modules:
  0.0 85.2 jit_solution(3017445065598328825)
XLA Ops:
  0.6 1.3 %load.1 = (bf16[528,1024]{1,0:T(8,128)(2,1)S(1)}, s32[1,512]{1,0:T(1,128)S(1)}, s32[1,512]{1,0:T(1,128)S(1)}) custom-call(bf16[512,1024]{1,0:T(8,128)(2,1)} %bitcast.9, s32[1,512]{1,0:T(1,128)} %seg_hbm.1, s32[1,512]{1,0:T(1,128)} %flag_hbm.1), custom_call_target="tpu_custom_call" | custom-call | flops 1 | bytes 1 | tf_op jit(solution)/shard_map/load/pallas_call | solution.py:350
  1.9 1.9 %collective-permute-start = (bf16[528,1024]{1,0:T(8,128)(2,1)S(1)}, bf16[528,1024]{1,0:T(8,128)(2,1)S(1)}, u32[]{:S(2)}, u32[]{:S(2)}) collective-permute-start(bf16[528,1024]{1,0:T(8,128)(2,1)S(1)} %get-tuple-element.41.x_ref), channel_id=1, source_target_pairs={{0,4},{4,8},{8,12},{12,16},{16,20},{20,24},{24,28},{28,32},{32,36}... | collective-permute-start | bytes 3244040 | tf_op jit(solution)/shard_map/ppermute | solution.py:405
  3.8 4.8 %collective-permute-start.1 = (bf16[1,512]{1,0:T(2,128)(2,1)}, bf16[1,512]{1,0:T(2,128)(2,1)S(1)}, u32[]{:S(2)}, u32[]{:S(2)}) collective-permute-start(bf16[1,512]{1,0:T(2,128)(2,1)} %param.17), channel_id=1, source_target_pairs={{0,0},{1,64},{2,128},{3,192},{64,1},{65,65},{66,129},{67,193},{128... | collective-permute-start | bytes 3080 | tf_op jit(solution)/shard_map/ppermute | solution.py:371
  8.8 4.7 %project.2 = (bf16[1024,1024]{1,0:T(8,128)(2,1)S(1)}, bf16[1024,1024]{1,0:T(8,128)(2,1)S(1)}, bf16[512,1024]{1,0:T(8,128)(2,1)S(1)}, bf16[512,1024]{1,0:T(8,128)(2,1)S(1)}) custom-call(s32[3]{0:T(128)S(1)} %pad_add_fusion.place_ref, bf16[528,1024]{1,0:T(8,128)(2,1)S(1)} %get-tuple-element.41.x_ref, bf16[1024,1024]{1,0:T(8,128)(2,1)} %refs_0_.2, ...), custom_call_target="tpu_custom_call" | custom-call | flops 1 | bytes 1 | tf_op jit(solution)/shard_map/project/pallas_call | solution.py:350
  13.5 1.8 %collective-permute-start.2 = (bf16[1,512]{1,0:T(2,128)(2,1)S(1)}, bf16[1,512]{1,0:T(2,128)(2,1)S(1)}, u32[]{:S(2)}, u32[]{:S(2)}) collective-permute-start(bf16[1,512]{1,0:T(2,128)(2,1)S(1)} %collective-permute-done.1.a_ref), channel_id=1, source_target_pairs={{0,4},{4,0},{1,5},{5,1},{2,6},{6,2},{3,7},{7,3},{8,12},{12,8},{9,1... | collective-permute-start | bytes 3080 | tf_op jit(solution)/shard_map/ppermute | solution.py:379
  15.3 0.8 collective-permute-done.2.b_ref
  16.3 3.2 %project.3 = (bf16[1024,1024]{1,0:T(8,128)(2,1)S(1)}, bf16[512,1024]{1,0:T(8,128)(2,1)S(1)}) custom-call(s32[3]{0:T(128)S(1)} %pad_add_fusion.place_ref, bf16[528,1024]{1,0:T(8,128)(2,1)S(1)} %get-tuple-element.41.x_ref, bf16[1024,1024]{1,0:T(8,128)(2,1)} %refs_0_.3), custom_call_target="tpu_custom_call" | custom-call | flops 1 | bytes 1 | tf_op jit(solution)/shard_map/project/pallas_call | solution.py:350
  19.8 4.6 %collective-permute-start.4 = (bf16[4,512]{1,0:T(4,128)(2,1)S(1)}, bf16[4,512]{1,0:T(4,128)(2,1)S(1)}, u32[]{:S(2)}, u32[]{:S(2)}) collective-permute-start(bf16[4,512]{1,0:T(4,128)(2,1)S(1)} %pad_maximum_fusion.1), channel_id=1, source_target_pairs={{0,16},{8,24},{16,0},{24,8},{32,48},{40,56},{48,32},{56,40},{1,17}... | collective-permute-start | bytes 12296 | tf_op jit(solution)/shard_map/ppermute | solution.py:379
  24.4 6.2 %near.1 = (f32[256,1024]{1,0:T(8,128)S(1)}, bf16[256,1024]{1,0:T(8,128)(2,1)S(1)}, bf16[256,1024]{1,0:T(8,128)(2,1)S(1)}, bf16[256,1024]{1,0:T(8,128)(2,1)S(1)}, bf16[1024,1024]{1,0:T(8,128)(2,1)S(1)}) custom-call(s32[3]{0:T(128)S(1)} %pad_add_fusion.place_ref, bf16[528,1024]{1,0:T(8,128)(2,1)S(1)} %collective-permute-done.xp_ref.marks_ref, ...), custom_call_target="tpu_custom_call" | custom-call | flops 1 | bytes 1 | tf_op jit(solution)/shard_map/near/pallas_call | solution.py:350
  30.6 3.3 %collective-permute-start.5 = (bf16[8,512]{1,0:T(8,128)(2,1)S(1)}, bf16[8,512]{1,0:T(8,128)(2,1)S(1)}, u32[]{:S(2)}, u32[]{:S(2)}) collective-permute-start(bf16[8,512]{1,0:T(8,128)(2,1)S(1)} %pad_maximum_fusion), channel_id=1, source_target_pairs={{0,32},{8,40},{16,48},{24,56},{32,0},{40,8},{48,16},{56,24},{1,33}... | collective-permute-start | bytes 24584 | tf_op jit(solution)/shard_map/ppermute | solution.py:379
  33.9 5.0 %far.1 = (f32[256,1024]{1,0:T(8,128)S(1)}, bf16[256,1024]{1,0:T(8,128)(2,1)S(1)}) custom-call(s32[3]{0:T(128)S(1)} %pad_add_fusion.place_ref, bf16[528,1024]{1,0:T(8,128)(2,1)S(1)} %collective-permute-done.xp_ref.marks_ref, bf16[1024,1024]{1,0:T(8,128)(2,1)S(1)} %get-tuple-element.38.wk_ref, bf16[1024,1024]{1,0:T(8,128)(2,1)S(1)} %get-tuple-element.42.wv_ref, ...), custom_call_target="tpu_custom_call" | custom-call | flops 1 | bytes 1 | tf_op jit(solution)/shard_map/far/pallas_call | solution.py:350
  39.0 0.6 query.1
  39.6 3.1 %pool.1 = (bf16[128,1152]{1,0:T(8,128)(2,1)S(1)}, bf16[128,1152]{1,0:T(8,128)(2,1)S(1)}, f32[512,1024]{1,0:T(8,128)}) custom-call(s32[3]{0:T(128)S(1)} %pad_add_fusion.place_ref, f32[256,1024]{1,0:T(8,128)S(1)} %get-tuple-element.58.low_ref, f32[256,1024]{1,0:T(8,128)S(1)} %get-tuple-element.59.high_ref, ...), custom_call_target="tpu_custom_call" | custom-call | flops 1 | bytes 1 | tf_op jit(solution)/shard_map/pool/pallas_call | solution.py:350
  42.9 1.6 %collective-permute-done.6.b_ref = bf16[128,1152]{1,0:T(8,128)(2,1)S(1)} collective-permute-done((bf16[128,1152]{1,0:T(8,128)(2,1)S(1)}, bf16[128,1152]{1,0:T(8,128)(2,1)S(1)}, u32[]{:S(2)}, u32[]{:S(2)}) %collective-permute-start.6) | collective-permute-done | bytes 294944 | tf_op jit(solution)/shard_map/ppermute | solution.py:379
  44.4 0.6 merge.1
  45.1 20.9 %all_to_all.5 = bf16[32,8,640]{2,1,0:T(8,128)(2,1)S(1)} all-to-all(bf16[32,8,640]{2,1,0:T(8,128)(2,1)S(1)} %bitcast.7), channel_id=1, replica_groups=mesh['y'=4,'z'=8,'core'=2,'x'=4] {'y','z'}, dimensions={0} | all-to-all | bytes 655360 | tf_op jit(solution)/shard_map/all_to_all | solution.py:440
  66.0 0.8 finish.1
  66.9 4.2 %collective-permute-start.7 = (f32[8,512]{1,0:T(8,128)S(1)}, f32[8,512]{1,0:T(8,128)S(1)}, u32[]{:S(2)}, u32[]{:S(2)}) collective-permute-start(f32[8,512]{1,0:T(8,128)S(1)} %finish.1), channel_id=1, source_target_pairs={{0,0},{1,64},{2,128},{3,192},{64,1},{65,65},{66,129},{67,193},{128... | collective-permute-start | bytes 49160 | tf_op jit(solution)/shard_map/ppermute | solution.py:371
  71.1 4.7 %collective-permute-done.7.row_ref = f32[8,512]{1,0:T(8,128)S(1)} collective-permute-done((f32[8,512]{1,0:T(8,128)S(1)}, f32[8,512]{1,0:T(8,128)S(1)}, u32[]{:S(2)}, u32[]{:S(2)}) %collective-permute-start.7) | collective-permute-done | bytes 16416 | tf_op jit(solution)/shard_map/ppermute | solution.py:371
  76.0 1.1 %collective-permute-start.10 = (f32[8,128]{1,0:T(8,128)S(1)}, f32[8,128]{1,0:T(8,128)S(1)}, u32[]{:S(2)}, u32[]{:S(2)}) collective-permute-start(f32[8,128]{1,0:T(8,128)S(1)} %rank.1.a_ref), channel_id=1, source_target_pairs={{0,3},{1,0},{2,1},{3,2},{4,7},{5,4},{6,5},{7,6},{8,11},{9,8},{10,9... | collective-permute-start | bytes 12296 | tf_op jit(solution)/shard_map/ppermute | solution.py:375
  77.1 2.2 %collective-permute-start.8 = (f32[8,128]{1,0:T(8,128)S(1)}, f32[8,128]{1,0:T(8,128)S(1)}, u32[]{:S(2)}, u32[]{:S(2)}) collective-permute-start(f32[8,128]{1,0:T(8,128)S(1)} %rank.1.a_ref), channel_id=1, source_target_pairs={{0,1},{1,2},{2,3},{3,0},{4,5},{5,6},{6,7},{7,4},{8,9},{9,10},{10,1... | collective-permute-start | bytes 12296 | tf_op jit(solution)/shard_map/ppermute | solution.py:375
  79.3 1.6 %collective-permute-done.10.d_ref = f32[8,128]{1,0:T(8,128)S(1)} collective-permute-done((f32[8,128]{1,0:T(8,128)S(1)}, f32[8,128]{1,0:T(8,128)S(1)}, u32[]{:S(2)}, u32[]{:S(2)}) %collective-permute-start.10) | collective-permute-done | bytes 4128 | tf_op jit(solution)/shard_map/ppermute | solution.py:375
  80.9 3.5 %collective-permute-done.9.c_ref = f32[8,128]{1,0:T(8,128)S(1)} collective-permute-done((f32[8,128]{1,0:T(8,128)S(1)}, f32[8,128]{1,0:T(8,128)S(1)}, u32[]{:S(2)}, u32[]{:S(2)}) %collective-permute-start.9) | collective-permute-done | bytes 4128 | tf_op jit(solution)/shard_map/ppermute | solution.py:375
  84.4 0.8 cross.1
  (27 shorter events, 0.9 us)
Async XLA Ops:
  1.9 22.5 %collective-permute-start = (bf16[528,1024]{1,0:T(8,128)(2,1)S(1)}, bf16[528,1024]{1,0:T(8,128)(2,1)S(1)}, u32[]{:S(2)}, u32[]{:S(2)}) collective-permute-start(bf16[528,1024]{1,0:T(8,128)(2,1)S(1)} %get-tuple-element.41.x_ref), channel_id=1, source_target_pairs={{0,4},{4,8},{8,12},{12,16},{16,20},{20,24},{24,28},{28,32},{32,36}... | collective-permute-start | bytes 3244040 | tf_op jit(solution)/shard_map/ppermute | solution.py:405
  3.8 9.6 %collective-permute-start.1 = (bf16[1,512]{1,0:T(2,128)(2,1)}, bf16[1,512]{1,0:T(2,128)(2,1)S(1)}, u32[]{:S(2)}, u32[]{:S(2)}) collective-permute-start(bf16[1,512]{1,0:T(2,128)(2,1)} %param.17), channel_id=1, source_target_pairs={{0,0},{1,64},{2,128},{3,192},{64,1},{65,65},{66,129},{67,193},{128... | collective-permute-start | bytes 3080 | tf_op jit(solution)/shard_map/ppermute | solution.py:371
  13.5 2.7 %collective-permute-start.2 = (bf16[1,512]{1,0:T(2,128)(2,1)S(1)}, bf16[1,512]{1,0:T(2,128)(2,1)S(1)}, u32[]{:S(2)}, u32[]{:S(2)}) collective-permute-start(bf16[1,512]{1,0:T(2,128)(2,1)S(1)} %collective-permute-done.1.a_ref), channel_id=1, source_target_pairs={{0,4},{4,0},{1,5},{5,1},{2,6},{6,2},{3,7},{7,3},{8,12},{12,8},{9,1... | collective-permute-start | bytes 3080 | tf_op jit(solution)/shard_map/ppermute | solution.py:379
  16.1 3.7 %collective-permute-start.3 = (bf16[2,512]{1,0:T(2,128)(2,1)S(1)}, bf16[2,512]{1,0:T(2,128)(2,1)S(1)}, u32[]{:S(2)}, u32[]{:S(2)}) collective-permute-start(bf16[2,512]{1,0:T(2,128)(2,1)S(1)} %pad_maximum_fusion.2), channel_id=1, source_target_pairs={{0,8},{8,0},{16,24},{24,16},{32,40},{40,32},{48,56},{56,48},{1,9},... | collective-permute-start | bytes 6152 | tf_op jit(solution)/shard_map/ppermute | solution.py:379
  19.8 10.8 %collective-permute-start.4 = (bf16[4,512]{1,0:T(4,128)(2,1)S(1)}, bf16[4,512]{1,0:T(4,128)(2,1)S(1)}, u32[]{:S(2)}, u32[]{:S(2)}) collective-permute-start(bf16[4,512]{1,0:T(4,128)(2,1)S(1)} %pad_maximum_fusion.1), channel_id=1, source_target_pairs={{0,16},{8,24},{16,0},{24,8},{32,48},{40,56},{48,32},{56,40},{1,17}... | collective-permute-start | bytes 12296 | tf_op jit(solution)/shard_map/ppermute | solution.py:379
  30.6 8.4 %collective-permute-start.5 = (bf16[8,512]{1,0:T(8,128)(2,1)S(1)}, bf16[8,512]{1,0:T(8,128)(2,1)S(1)}, u32[]{:S(2)}, u32[]{:S(2)}) collective-permute-start(bf16[8,512]{1,0:T(8,128)(2,1)S(1)} %pad_maximum_fusion), channel_id=1, source_target_pairs={{0,32},{8,40},{16,48},{24,56},{32,0},{40,8},{48,16},{56,24},{1,33}... | collective-permute-start | bytes 24584 | tf_op jit(solution)/shard_map/ppermute | solution.py:379
  33.9 5.1 %copy-start.1 = (bf16[512,1024]{1,0:T(8,128)(2,1)S(1)}, bf16[512,1024]{1,0:T(8,128)(2,1)}, u32[]{:S(2)}) copy-start(bf16[512,1024]{1,0:T(8,128)(2,1)} %pers_ref.1) | copy-start | bytes 3145732
  33.9 5.1 %copy-start.4 = (bf16[16,1024]{1,0:T(8,128)(2,1)S(1)}, bf16[16,1024]{1,0:T(8,128)(2,1)}, u32[]{:S(2)}) copy-start(bf16[16,1024]{1,0:T(8,128)(2,1)} %seed_ref.1) | copy-start | bytes 98308
  42.7 23.3 %copy-start = (bf16[1024,512]{1,0:T(8,128)(2,1)S(1)}, bf16[1024,512]{1,0:T(8,128)(2,1)}, u32[]{:S(2)}) copy-start(bf16[1024,512]{1,0:T(8,128)(2,1)} %comp_ref.1) | copy-start | bytes 3145732
  42.7 33.1 %copy-start.2 = (bf16[2048,128]{1,0:T(8,128)(2,1)S(1)}, bf16[2048,128]{1,0:T(8,128)(2,1)}, u32[]{:S(2)}) copy-start(bf16[2048,128]{1,0:T(8,128)(2,1)} %down_ref.1) | copy-start | bytes 1572868
  42.8 36.6 %copy-start.5 = (bf16[2048]{0:T(1024)(128)(2,1)S(1)}, bf16[2048]{0:T(1024)(128)(2,1)}, u32[]{:S(2)}) copy-start(bf16[2048]{0:T(1024)(128)(2,1)} %param.27) | copy-start | bytes 12292
  42.8 41.7 %copy-start.3 = (bf16[128,2048]{1,0:T(8,128)(2,1)S(1)}, bf16[128,2048]{1,0:T(8,128)(2,1)}, u32[]{:S(2)}) copy-start(bf16[128,2048]{1,0:T(8,128)(2,1)} %up_ref.1) | copy-start | bytes 1572868
  42.8 1.7 %collective-permute-start.6 = (bf16[128,1152]{1,0:T(8,128)(2,1)S(1)}, bf16[128,1152]{1,0:T(8,128)(2,1)S(1)}, u32[]{:S(2)}, u32[]{:S(2)}) collective-permute-start(bf16[128,1152]{1,0:T(8,128)(2,1)S(1)} %get-tuple-element.71), channel_id=1, source_target_pairs={{0,4},{4,0},{1,5},{5,1},{2,6},{6,2},{3,7},{7,3},{8,12},{12,8},{9,1... | collective-permute-start | bytes 884744 | tf_op jit(solution)/shard_map/ppermute | solution.py:379
  66.9 8.9 %collective-permute-start.7 = (f32[8,512]{1,0:T(8,128)S(1)}, f32[8,512]{1,0:T(8,128)S(1)}, u32[]{:S(2)}, u32[]{:S(2)}) collective-permute-start(f32[8,512]{1,0:T(8,128)S(1)} %finish.1), channel_id=1, source_target_pairs={{0,0},{1,64},{2,128},{3,192},{64,1},{65,65},{66,129},{67,193},{128... | collective-permute-start | bytes 49160 | tf_op jit(solution)/shard_map/ppermute | solution.py:371
  76.0 4.9 %collective-permute-start.10 = (f32[8,128]{1,0:T(8,128)S(1)}, f32[8,128]{1,0:T(8,128)S(1)}, u32[]{:S(2)}, u32[]{:S(2)}) collective-permute-start(f32[8,128]{1,0:T(8,128)S(1)} %rank.1.a_ref), channel_id=1, source_target_pairs={{0,3},{1,0},{2,1},{3,2},{4,7},{5,4},{6,5},{7,6},{8,11},{9,8},{10,9... | collective-permute-start | bytes 12296 | tf_op jit(solution)/shard_map/ppermute | solution.py:375
  77.1 3.8 %collective-permute-start.8 = (f32[8,128]{1,0:T(8,128)S(1)}, f32[8,128]{1,0:T(8,128)S(1)}, u32[]{:S(2)}, u32[]{:S(2)}) collective-permute-start(f32[8,128]{1,0:T(8,128)S(1)} %rank.1.a_ref), channel_id=1, source_target_pairs={{0,1},{1,2},{2,3},{3,0},{4,5},{5,6},{6,7},{7,4},{8,9},{9,10},{10,1... | collective-permute-start | bytes 12296 | tf_op jit(solution)/shard_map/ppermute | solution.py:375
  79.3 5.1 %collective-permute-start.9 = (f32[8,128]{1,0:T(8,128)S(1)}, f32[8,128]{1,0:T(8,128)S(1)}, u32[]{:S(2)}, u32[]{:S(2)}) collective-permute-start(f32[8,128]{1,0:T(8,128)S(1)} %rank.1.a_ref), channel_id=1, source_target_pairs={{0,2},{1,3},{2,0},{3,1},{4,6},{5,7},{6,4},{7,5},{8,10},{9,11},{10,... | collective-permute-start | bytes 12296 | tf_op jit(solution)/shard_map/ppermute | solution.py:375
